TPU v7x, 256 devices: a whole 4x4x8 slice. The times are simulated.
256 devices in a mesh: wide: 32 (over x_lo, z, core), head: 8 (over y, x_hi).
Axes of the slice: x: 4 (x_hi: 2, x_lo: 2; x = x_hi * 2 + x_lo), y: 4, z: 8, core: 2. Of those that a mesh axis runs over, the one named last changes fastest.
Arguments:
- tokens: bfloat16 [32, 1024, 4096], P('wide'), may hold values from -6 to 6
- slab_index: int32 [32], P('wide'), may hold values from 0 to 3
- agg_query: bfloat16 [4096], P('head'), may hold values from -360 to 360
- agg_key_w: bfloat16 [4096, 4096], P('wide', 'head'), may hold values from -0.09375 to 0.09375
- agg_value_w: bfloat16 [4096, 4096], P('wide', 'head'), may hold values from -0.09375 to 0.09375
- agg_out_w: bfloat16 [4096, 4096], P('head', 'wide'), may hold values from -0.09375 to 0.09375
- norm_gain: float32 [4096], replicated, may hold values from 0.9 to 8
- query_w: bfloat16 [4096, 4096], P('wide', 'head'), may hold values from -0.09375 to 0.09375
- key_w: bfloat16 [4096, 4096], P('wide', 'head'), may hold values from -0.09375 to 0.09375
- value_w: bfloat16 [4096, 4096], P('wide', 'head'), may hold values from -0.09375 to 0.09375
Outputs:
- attended: bfloat16 [256, 4096], P('wide', 'head')
All inputs are finite; a program needn't handle non-finite values.
Results may differ from a plain program's by a relative error of at most 0.035.
Values may be sent and summed in bfloat16 or wider, within the bound.
No kernel may reach another device: no remote copies, remote signals or barrier semaphores. Data moves between devices by JAX's collectives and lax.ppermute only.
A program may use at most 192 MiB of HBM per device.

v0:
```python
import math

import jax
import jax.numpy as jnp
from jax import lax
from jax.sharding import PartitionSpec as P

HEADS = 32
Q_DEV = 8


def normalize(rows, norm_gain):
    values_f = rows.astype(jnp.float32)
    row_mean = jnp.mean(values_f, axis=-1, keepdims=True)
    centred = values_f - row_mean
    row_var = jnp.mean(centred * centred, axis=-1, keepdims=True)
    return (centred * lax.rsqrt(row_var + 1e-05) * norm_gain).astype(jnp.bfloat16)


def on_device(
    tokens,
    slab_index,
    agg_query,
    agg_key_w,
    agg_value_w,
    agg_out_w,
    norm_gain,
    query_w,
    key_w,
    value_w,
):
    highest_precision = lax.Precision.HIGHEST
    n_wide = lax.axis_size("wide")
    model = tokens.shape[2]
    columns = agg_key_w.shape[1]
    head_dim = model // HEADS
    heads_here = columns // head_dim
    factor = 1.0 / math.sqrt(head_dim)
    loc_dev = tokens.shape[1] // n_wide
    variable_token_rows = lax.all_to_all(tokens, "wide", split_axis=1, concat_axis=0, tiled=True)
    variables = variable_token_rows.shape[0]
    flattened = variable_token_rows.reshape(variables * loc_dev, model)
    query_vec = agg_query.astype(jnp.float32).reshape(heads_here, head_dim)
    key_proj = jnp.dot(
        flattened,
        lax.all_gather(agg_key_w, "wide", axis=0, tiled=True),
        preferred_element_type=jnp.float32,
    )
    aggregate_logits = (
        jnp.einsum(
            "rhj,hj->rh",
            key_proj.reshape(-1, heads_here, head_dim),
            query_vec,
            precision=highest_precision,
        )
        * factor
    )
    aggregate_probabilities = jax.nn.softmax(
        aggregate_logits.reshape(variables, loc_dev, heads_here), axis=0
    )
    pooled_tokens = jnp.einsum(
        "ybz,ybw->bzw",
        aggregate_probabilities,
        variable_token_rows.astype(jnp.float32),
        precision=highest_precision,
    )
    weights_piece = lax.all_gather(agg_value_w, "wide", axis=0, tiled=True)
    piece_rows = weights_piece.shape[0]
    piece_f = weights_piece.astype(jnp.float32).reshape(piece_rows, heads_here, head_dim)
    head_out = jnp.einsum("lhd,dhj->lhj", pooled_tokens, piece_f, precision=highest_precision)
    agg_heads = head_out.reshape(loc_dev, columns).astype(jnp.bfloat16)
    partial_sum = jnp.dot(
        agg_heads,
        lax.all_gather(agg_out_w, "wide", axis=1, tiled=True),
        preferred_element_type=jnp.float32,
    )
    aggregated = lax.psum(partial_sum, "head").astype(jnp.bfloat16)
    normed = normalize(aggregated, norm_gain)
    slab_rows = lax.dynamic_slice_in_dim(normed, slab_index[0] * Q_DEV, Q_DEV, 0)
    pieces = (
        lax.all_gather(query_w, "wide", axis=0, tiled=True),
        lax.all_gather(key_w, "wide", axis=0, tiled=True),
        lax.all_gather(value_w, "wide", axis=0, tiled=True),
    )
    query_acc = jnp.dot(slab_rows, pieces[0], preferred_element_type=jnp.float32)
    key_acc = jnp.dot(normed, pieces[1], preferred_element_type=jnp.float32)
    value_acc = jnp.dot(normed, pieces[2], preferred_element_type=jnp.float32)
    query_f = (
        query_acc.astype(jnp.bfloat16).astype(jnp.float32).reshape(Q_DEV, heads_here, head_dim)
    )
    key_out = key_acc.astype(jnp.bfloat16)
    value_out = value_acc.astype(jnp.bfloat16)
    pieces = (
        lax.all_gather(key_out, "wide", axis=0, tiled=True),
        lax.all_gather(value_out, "wide", axis=0, tiled=True),
    )
    running_top = jnp.full((heads_here, Q_DEV), -jnp.inf, jnp.float32)
    running_sum = jnp.zeros((heads_here, Q_DEV), jnp.float32)
    accum = jnp.zeros((heads_here, Q_DEV, head_dim), jnp.float32)
    key_piece = pieces[0].astype(jnp.float32).reshape(-1, heads_here, head_dim)
    value_piece = pieces[1].astype(jnp.float32).reshape(-1, heads_here, head_dim)
    scores = jnp.einsum("qhj,khj->hqk", query_f, key_piece, precision=highest_precision) * factor
    new_top = jnp.max(scores, axis=-1)
    fading = jnp.exp(running_top - new_top)
    weights_now = jnp.exp(scores - new_top[..., None])
    running_sum = running_sum * fading + jnp.sum(weights_now, axis=-1)
    accum = accum * fading[..., None] + jnp.einsum(
        "hqk,khj->hqj", weights_now, value_piece, precision=highest_precision
    )
    attended = accum / running_sum[..., None]
    return jnp.transpose(attended, (1, 0, 2)).reshape(Q_DEV, columns).astype(jnp.bfloat16)


def solution(mesh):
    placed = (
        P("wide", None, None),
        P("wide"),
        P("head"),
        P("wide", "head"),
        P("wide", "head"),
        P("head", "wide"),
        P(),
        P("wide", "head"),
        P("wide", "head"),
        P("wide", "head"),
    )
    return jax.shard_map(
        on_device, mesh=mesh, in_specs=placed, out_specs=P("wide", "head"), check_vma=False
    )
```

profile of v0, /device:TPU:1, one launch (start us, length us, event | category | flops | bytes accessed | tf_op | source)
XLA Modules:
  0.0 697.2 jit_solution(6215420640961428701)
XLA Ops:
  6.5 0.0 copy-start
  6.5 0.0 all-gather.9.cloned.1.call-start
  6.5 0.7 all-gather.9.cloned.1.call-update
  7.3 0.0 all-gather.11.cloned.1.call-start
  7.3 1.7 copy.30
  9.0 0.0 all-gather.11.cloned.1.call-update
  9.0 0.0 all-gather.13.cloned.1.call-start
  9.0 0.7 all-gather.13.cloned.1.call-update
  9.7 0.0 all-gather.17.cloned.1.call-start
  9.8 0.5 all-gather.17.cloned.1.call-update
  10.3 20.1 %copy.70 = bf16[1,1024,4096]{2,0,1:T(2,128)(2,1)} copy(bf16[1,1024,4096]{2,1,0:T(8,128)(2,1)} %param.10) | data formatting | bytes 16777216 | tf_op args[0]
  30.4 0.5 broadcast.52
  30.9 53.6 %reduce = bf16[1024,4096]{1,0:T(8,128)(2,1)} reduce(bf16[1024,1,4096]{2,1,0:T(2,128)(2,1)} %bitcast.79, bf16[]{:T(256)} %broadcast.52), dimensions={1}, to_apply=%bitcast.76.reduce_sub_computation | reduce | bytes 16777218
  84.5 21.6 %reshape.71 = bf16[32,2,65536]{2,1,0:T(2,128)(2,1)} reshape(bf16[1024,4096]{1,0:T(8,128)(2,1)} %reduce) | data formatting | bytes 16777216
  106.2 11.2 %all-to-all-start = ((bf16[32,2,65536]{2,1,0:T(2,128)(2,1)}), bf16[32,2,65536]{2,1,0:T(2,128)(2,1)}, u32[]{:S(2)}, u32[]{:S(2)}) async-start(bf16[32,2,65536]{2,1,0:T(2,128)(2,1)} %reshape.71), calls=%async_computation | async-start | bytes 16777216 | tf_op jit(solution)/shard_map/all_to_all | solution.py:40
  117.3 0.0 all-gather.21.cloned.1.call-start
  117.4 0.5 all-gather.21.cloned.1.call-update
  117.9 0.0 all-gather.15.cloned.1.call-start
  118.0 0.5 all-gather.15.cloned.1.call-update
  118.5 0.2 all-gather.19.cloned.1.call-start
  118.7 0.0 all-gather.9.cloned.1.call-done
  118.7 6.4 copy.27
  125.2 198.3 %all-to-all-done = bf16[32,2,65536]{2,1,0:T(2,128)(2,1)} async-done(((bf16[32,2,65536]{2,1,0:T(2,128)(2,1)}), bf16[32,2,65536]{2,1,0:T(2,128)(2,1)}, u32[]{:S(2)}, u32[]{:S(2)}) %all-to-all-start) | async-done | bytes 8388640 | tf_op jit(solution)/shard_map/all_to_all | solution.py:40
  323.5 23.4 %reshape.72 = bf16[1024,1,4096]{2,1,0:T(2,128)(2,1)} reshape(bf16[32,2,65536]{2,1,0:T(2,128)(2,1)} %all-to-all-done) | data formatting | bytes 16777216
  346.9 0.0 copy-start.2
  346.9 15.7 %copy.39 = bf16[1,1024,4096]{2,1,0:T(8,128)(2,1)S(1)} copy(bf16[1,1024,4096]{2,0,1:T(2,128)(2,1)} %bitcast.78) | data formatting | bytes 16777216
  362.6 0.0 copy-start.1
  362.6 0.0 copy-done.2
  362.6 4.5 fusion.1
  367.2 0.0 copy-done.1
  367.2 0.0 copy-done
  367.2 1.0 fusion.36
  368.3 0.1 reshape.62
  368.3 0.1 fusion.39
  368.5 0.1 copy.28
  368.6 16.9 %fusion.3 = f32[32,4,4096]{2,1,0:T(4,128)S(1)} fusion(f32[32,32,4]{0,2,1:T(4,128)S(1)} %copy.28, bf16[32,32,4096]{2,1,0:T(8,128)(2,1)} %bitcast.80), kind=kOutput, calls=%fused_computation.3 | convolution fusion | flops 201326592 | bytes 10502144 | tf_op jit(solution)/shard_map/ybz,ybw->bzw/dot_general | solution.py:61
  385.5 0.0 all-gather.11.cloned.1.call-done
  385.6 6.1 fusion.12
  391.7 0.0 copy-start.3
  391.7 0.0 all-gather.13.cloned.1.call-done
  391.7 3.0 fusion.32
  394.7 50.8 %all-reduce.1 = bf16[32,4096]{1,0:T(8,128)(2,1)S(1)} all-reduce(f32[32,4096]{1,0:T(8,128)S(1)} %fusion.32), channel_id=1, replica_groups=mesh['wide'=32,'head'=8] {'head'}, use_global_device_ids=true, to_apply=%region_2.0 | all-reduce | flops 131072 | bytes 786432 | tf_op jit(solution)/shard_map/psum | solution.py:77
  445.5 0.2 convert_reduce_fusion
  445.7 0.3 fusion.26
  445.9 0.0 copy-done.3
  446.0 0.1 fusion.28
  446.1 0.0 all-gather.17.cloned.1.call-done
  446.1 3.7 convolution_convert_fusion.1
  449.8 0.0 all-gather.19.cloned.1.call-update
  449.8 0.0 all-gather.23.cloned.1.call-start
  449.9 39.7 %all-gather.21.cloned.1.call-done = bf16[4096,512]{1,0:T(8,128)(2,1)} async-done(((bf16[128,512]{1,0:T(8,128)(2,1)}), bf16[4096,512]{1,0:T(8,128)(2,1)}) %all-gather.21.cloned.1.call-update) | async-done | bytes 4194320 | tf_op jit(solution)/shard_map/all_gather | solution.py:83
  489.6 3.6 convolution_convert_fusion
  493.2 0.0 all-gather.23.cloned.1.call-update
  493.9 63.8 %all-gather.15.cloned.1.call-done = bf16[4096,512]{1,0:T(8,128)(2,1)} async-done(((bf16[128,512]{1,0:T(8,128)(2,1)}), bf16[4096,512]{1,0:T(8,128)(2,1)}) %all-gather.15.cloned.1.call-update) | async-done | bytes 4194320 | tf_op jit(solution)/shard_map/all_gather | solution.py:81
  557.7 2.8 fusion.18
  560.5 62.3 %all-gather.19.cloned.1.call-done = bf16[1024,512]{1,0:T(8,128)(2,1)} async-done(((bf16[32,512]{1,0:T(8,128)(2,1)}), bf16[1024,512]{1,0:T(8,128)(2,1)}) %all-gather.19.cloned.1.call-update) | async-done | bytes 1048592 | tf_op jit(solution)/shard_map/all_gather | solution.py:94
  622.8 1.7 fusion.40
  624.5 0.2 fusion.29
  624.7 63.3 %all-gather.23.cloned.1.call-done = bf16[1024,512]{1,0:T(8,128)(2,1)} async-done(((bf16[32,512]{1,0:T(8,128)(2,1)}), bf16[1024,512]{1,0:T(8,128)(2,1)}) %all-gather.23.cloned.1.call-update) | async-done | bytes 1048592 | tf_op jit(solution)/shard_map/all_gather | solution.py:95
  688.0 2.4 fusion.19
  (6 shorter events, 0.1 us)
Async XLA Ops:
  6.5 360.6 %copy-start = (bf16[512]{0:T(512)(128)(2,1)S(1)}, bf16[512]{0:T(512)(128)(2,1)}, u32[]{:S(2)}) copy-start(bf16[512]{0:T(512)(128)(2,1)} %param.12) | copy-start | bytes 3076
  6.5 112.2 %all-gather.9.cloned.1.call-start = ((), (), s32[]{:S(2)}) async-start(), calls=%async_computation.1 | async-start | bytes 4325376 | tf_op jit(solution)/shard_map/all_gather | solution.py:46
  7.3 378.3 %all-gather.11.cloned.1.call-start = ((), (), s32[]{:S(2)}) async-start(), calls=%async_computation.2 | async-start | bytes 4325376 | tf_op jit(solution)/shard_map/all_gather | solution.py:67
  9.0 382.7 %all-gather.13.cloned.1.call-start = ((), (), s32[]{:S(2)}) async-start(), calls=%async_computation.3 | async-start | bytes 4325376 | tf_op jit(solution)/shard_map/all_gather | solution.py:74
  9.7 436.4 %all-gather.17.cloned.1.call-start = ((), (), s32[]{:S(2)}) async-start(), calls=%async_computation.5 | async-start | bytes 4325376 | tf_op jit(solution)/shard_map/all_gather | solution.py:82
  106.2 217.3 %all-to-all-start = ((bf16[32,2,65536]{2,1,0:T(2,128)(2,1)}), bf16[32,2,65536]{2,1,0:T(2,128)(2,1)}, u32[]{:S(2)}, u32[]{:S(2)}) async-start(bf16[32,2,65536]{2,1,0:T(2,128)(2,1)} %reshape.71), calls=%async_computation | async-start | bytes 16777216 | tf_op jit(solution)/shard_map/all_to_all | solution.py:40
  117.3 372.2 %all-gather.21.cloned.1.call-start = ((), (), s32[]{:S(2)}) async-start(), calls=%async_computation.7 | async-start | bytes 4325376 | tf_op jit(solution)/shard_map/all_gather | solution.py:83
  117.9 439.8 %all-gather.15.cloned.1.call-start = ((), (), s32[]{:S(2)}) async-start(), calls=%async_computation.4 | async-start | bytes 4325376 | tf_op jit(solution)/shard_map/all_gather | solution.py:81
  118.5 504.3 %all-gather.19.cloned.1.call-start = ((), (), s32[]{:S(2)}) async-start(), calls=%async_computation.6 | async-start | bytes 1081344 | tf_op jit(solution)/shard_map/all_gather | solution.py:94
  346.9 15.7 %copy-start.2 = (bf16[512,4096]{1,0:T(8,128)(2,1)S(1)}, bf16[512,4096]{1,0:T(8,128)(2,1)}, u32[]{:S(2)}) copy-start(bf16[512,4096]{1,0:T(8,128)(2,1)} %copy.27) | copy-start | bytes 12582916
  362.6 4.5 copy-start.1
  391.7 54.3 %copy-start.3 = (f32[4096]{0:T(1024)S(1)}, f32[4096]{0:T(1024)}, u32[]{:S(2)}) copy-start(f32[4096]{0:T(1024)} %param.16) | copy-start | bytes 49156
  449.8 238.1 %all-gather.23.cloned.1.call-start = ((), (), s32[]{:S(2)}) async-start(), calls=%async_computation.8 | async-start | bytes 1081344 | tf_op jit(solution)/shard_map/all_gather | solution.py:95
Sparse Core Ops, SparseCore 0:
  9.2 71.0 all-gather.8
  82.0 120.5 all-gather.10
  204.4 149.3 all-gather.12
  355.5 65.6 all-gather.16
  422.9 66.6 all-gather.20
  491.3 66.3 all-gather.14
  559.5 63.2 all-gather.18
  624.6 63.2 all-gather.22
where the time goes:
time: 699 us; the launch traced here: 697 us
  waiting for transfers between devices  430 us (62%)
  local copies, waits for them, and re-layouts  89.6 us (13%)
  other arithmetic  54.6 us (8%)
  blocking collectives  50.8 us (7%)
  matrix products  45.9 us (7%)
  between operations  14.3 us (2%)
  starting transfers between devices  11.6 us (2%)
    all_to_all x1, waiting for transfers between devices, on_device(): lax.all_to_all(tokens, 'wide', split_axis=1, concat_axis=0, tiled=True)  198 us
    unnamed x14, local copies, waits for them, and re-layouts  83 us
    all_gather x1, waiting for transfers between devices, on_device(): lax.all_gather(query_w, 'wide', axis=0, tiled=True)  63.8 us
    all_gather x1, waiting for transfers between devices, on_device(): lax.all_gather(value_out, 'wide', axis=0, tiled=True)  63.3 us
    all_gather x1, waiting for transfers between devices, on_device(): lax.all_gather(key_out, 'wide', axis=0, tiled=True)  62.3 us
    unnamed x1, other arithmetic  53.6 us
    psum x1, blocking collectives, on_device(): aggregated = lax.psum(partial_sum, 'head').astype(jnp.bfloat16)  50.8 us
    all_gather x1, waiting for transfers between devices, on_device(): lax.all_gather(value_w, 'wide', axis=0, tiled=True)  39.7 us
  transfers between devices with their start and end apart: 9, of which 5 were waited for; matrix products, arithmetic and copies ran while one was open for 27% of the time, Pallas kernels for 0%

commit v1 on v0

v1 whole, which is shorter than its diff:
```python
import functools
import math

import jax
import jax.numpy as jnp
from jax import lax
from jax.experimental import pallas as pl
from jax.experimental.pallas import tpu as pltpu
from jax.sharding import Mesh, PartitionSpec as P

HEADS = 32
Q_DEV = 8
F32 = jnp.float32
BF16 = jnp.bfloat16
WIDE = ("xl", "z", "c")
HEAD = ("y", "xh")
LANES = 128
PARTS = 16
NT = (((1,), (1,)), ((), ()))
VMEM_BYTES = 48 * 1024 * 1024


def call(body, pos, out_shape, in_specs, out_specs, args, grid=(1,), scratch=(), flops=0, aliases=None):
    shapes = out_shape if isinstance(out_shape, (list, tuple)) else [out_shape]
    moved = sum(a.size * a.dtype.itemsize for a in args) + sum(math.prod(s.shape) * s.dtype.itemsize for s in shapes)
    return pl.pallas_call(
        body,
        out_shape=out_shape,
        grid_spec=pltpu.PrefetchScalarGridSpec(
            num_scalar_prefetch=1, grid=grid, in_specs=in_specs, out_specs=out_specs, scratch_shapes=list(scratch)
        ),
        input_output_aliases=aliases or {},
        compiler_params=pltpu.CompilerParams(vmem_limit_bytes=VMEM_BYTES),
        cost_estimate=pl.CostEstimate(flops=flops, bytes_accessed=moved, transcendentals=0),
    )(pos, *args)


def full(shape):
    return pl.BlockSpec(shape, lambda i, s: (0,) * len(shape))


def sds(shape, dtype):
    return jax.ShapeDtypeStruct(shape, dtype)


def lane(shape):
    return lax.broadcasted_iota(jnp.int32, shape, len(shape) - 1)


def rounded(x):
    return x.astype(BF16).astype(F32)


def pack_body(heads, factor, pos, q_ref, key_ref, value_ref, out_ref):
    columns = key_ref.shape[1]
    rows = key_ref.shape[0]
    head_dim = columns // heads
    row = lax.broadcasted_iota(jnp.int32, (PARTS, columns), 0)
    col = lane((PARTS, columns))
    q = jnp.broadcast_to(q_ref[...].astype(F32), (PARTS, columns))
    q_diag = jnp.where(lax.rem(row, heads) == lax.div(col, head_dim), q, 0.0).astype(BF16)
    merged = factor * lax.dot_general(q_diag, key_ref[...], NT, preferred_element_type=F32)
    hi = rounded(merged)
    mid = rounded(merged - hi)
    low = merged - hi - mid
    r = lax.broadcasted_iota(jnp.int32, merged.shape, 0)
    parts = jnp.where(r < heads, hi, jnp.where(r < 2 * heads, mid, jnp.where(r < 3 * heads, low, 0.0)))
    out_ref[:rows, :] = value_ref[...]
    out_ref[rows:, :] = jnp.concatenate([parts, jnp.zeros((PARTS, columns - rows), F32)], 1).astype(BF16)


def fold(x, heads):
    total = x + pltpu.roll(x, LANES - heads, 1) + pltpu.roll(x, LANES - 2 * heads, 1)
    return jnp.where(lane(x.shape) < heads, total, 0.0)


def unfold(s, heads):
    s = jnp.where(lane(s.shape) < heads, s, 0.0)
    hi = rounded(s)
    mid = rounded(s - hi)
    low = s - hi - mid
    return (hi + pltpu.roll(mid, heads, 1) + pltpu.roll(low, 2 * heads, 1)).astype(BF16)


def widen(p, heads, head_dim):
    return jnp.concatenate([jnp.broadcast_to(p[:, h : h + 1], (p.shape[0], head_dim)) for h in range(heads)], 1)


def merge(v0, s0, v1, s1, heads, head_dim):
    top = jnp.maximum(s0, s1)
    e0, e1 = jnp.exp(s0 - top), jnp.exp(s1 - top)
    total = e0 + e1
    v = widen(e0 / total, heads, head_dim) * v0 + widen(e1 / total, heads, head_dim) * v1.astype(F32)
    return v, top + jnp.log(total)


def value_body(n_chunks, first, last, heads, pos, *refs):
    tok = refs[: 4 * n_chunks]
    blocks = refs[4 * n_chunks : 6 * n_chunks]
    rest = refs[6 * n_chunks :]
    rows = tok[0].shape[1] if len(tok[0].shape) == 3 else tok[0].shape[0]
    d = tok[0].shape[-1]
    lhs = jnp.concatenate([t[...].reshape(rows, d) for t in tok], 1)
    pieces = [b[x] for i in range(n_chunks) for b in blocks[2 * i : 2 * i + 2] for x in (0, 1)]
    rhs = jnp.concatenate([p[:d] for p in pieces], 0)
    parts = jnp.concatenate([p[d:, :d] for p in pieces], 1)
    v = jnp.dot(lhs, rhs, preferred_element_type=F32)
    s = lax.dot_general(lhs, parts, NT, preferred_element_type=F32)
    s = jnp.concatenate([s, jnp.zeros((rows, LANES - PARTS), F32)], 1)
    if not first:
        v = v + rest[0][...]
        s = s + rest[1][...]
        rest = rest[2:]
    if not last:
        rest[0][...] = v
        rest[1][...] = s
        return
    msg_ref, v_ref, s_ref = rest
    groups, loc_dev, width = v_ref.shape
    s = fold(s, heads)
    v4 = v.reshape(groups, 2, loc_dev, width)
    s4 = s.reshape(groups, 2, loc_dev, LANES)
    p4 = unfold(s, heads).astype(F32).reshape(groups, 2, loc_dev, LANES)
    even = pos[0] == 0
    v_ref[...] = jnp.where(even, v4[:, 0], v4[:, 1])
    s_ref[...] = jnp.where(even, s4[:, 0], s4[:, 1])
    msg_ref[:, :, :width] = jnp.where(even, v4[:, 1], v4[:, 0]).astype(BF16)
    msg_ref[:, :, width:] = jnp.where(even, p4[:, 1], p4[:, 0]).astype(BF16)


def value_call(pos, toks, chunks, acc, last, heads, loc_dev, tile=256):
    locs, model = toks.shape
    n = len(chunks)
    width = chunks[0][1].shape[2]
    d = chunks[0][1].shape[1] - PARTS
    half = model // (2 * d)
    in_specs, args = [], []
    for slot, _, _ in chunks:
        for flip in (0, 1):
            for x in (0, 1):
                def place(i, s, slot=slot, flip=flip, x=x):
                    core = s[0] if flip == 0 else 1 - s[0]
                    return i, x * half + 2 * s[slot] + core
                in_specs.append(pl.BlockSpec((tile, d), place))
                args.append(toks)
    for _, own, other in chunks:
        in_specs += [full(own.shape)] * 2
        args += [own, other]
    rows2 = [pl.BlockSpec((tile, width), lambda i, s: (i, 0)), pl.BlockSpec((tile, LANES), lambda i, s: (i, 0))]
    aliases = None
    if acc is not None:
        if not last:
            aliases = {1 + len(args): 0, 2 + len(args): 1}
        in_specs += rows2
        args += list(acc)
    if last:
        g = tile // (2 * loc_dev)
        total = locs // (2 * loc_dev)
        shapes = [(total, loc_dev, width + LANES), (total, loc_dev, width), (total, loc_dev, LANES)]
        out_shape = [sds(sh, t) for sh, t in zip(shapes, (BF16, F32, F32))]
        out_specs = [pl.BlockSpec((g,) + sh[1:], lambda i, s: (i, 0, 0)) for sh in shapes]
    else:
        out_shape = [sds((locs, width), F32), sds((locs, LANES), F32)]
        out_specs = rows2
    body = functools.partial(value_body, n, acc is None, last, heads)
    flops = 2 * locs * 4 * n * d * width
    return call(body, pos, out_shape, in_specs, out_specs, args, grid=(locs // tile,), flops=flops, aliases=aliases)


def core_body(heads, pos, v_ref, s_ref, msg_ref, send_ref, v_out, s_out):
    width = v_ref.shape[-1]
    head_dim = width // heads
    for mine in (False, True):
        half = pos[1] if mine else 1 - pos[1]
        v, s = merge(
            v_ref[half],
            s_ref[half],
            msg_ref[half, :, :width],
            fold(msg_ref[half, :, width:].astype(F32), heads),
            heads,
            head_dim,
        )
        if mine:
            v_out[...] = v
            s_out[...] = s
        else:
            send_ref[:, :width] = v.astype(BF16)
            send_ref[:, width:] = unfold(s, heads)


def pair_body(heads, pos, v_ref, s_ref, msg_ref, out_ref):
    width = v_ref.shape[-1]
    s1 = fold(msg_ref[:, width:].astype(F32), heads)
    v, s = merge(v_ref[...], s_ref[...], msg_ref[:, :width], s1, heads, width // heads)
    out_ref[:, :width] = v.astype(BF16)
    out_ref[:, width:] = unfold(s, heads)


def ring_body(heads, pos, msg_ref, out_ref, scratch):
    n, rows, width = msg_ref.shape
    width -= LANES
    logs = [fold(msg_ref[i, :, width:].astype(F32), heads) for i in range(n)]
    top = functools.reduce(jnp.maximum, logs)
    powers = [jnp.exp(s - top) for s in logs]
    total = functools.reduce(jnp.add, powers)
    out = jnp.zeros((rows, width), F32)
    for i in range(n):
        out += widen(powers[i] / total, heads, width // heads) * msg_ref[i, :, :width].astype(F32)
    scratch[:rows, :] = out
    scratch[rows:, :] = out
    start = pl.multiple_of(pos[6] * Q_DEV, Q_DEV)
    out_ref[...] = scratch[pl.ds(start, rows), :].astype(BF16)


def out_body(pos, own_ref, far_ref, w_ref, out_ref, scratch):
    c, xl = pos[0], pos[1]
    for ref, side in ((own_ref, xl), (far_ref, 1 - xl)):
        scratch[2 * side + c] = ref[0]
        scratch[2 * side + 1 - c] = ref[1]
    rows = scratch.shape[0] * scratch.shape[1]
    a = scratch[...].reshape(rows, scratch.shape[2])
    n, _, width = w_ref.shape
    groups, per, _ = out_ref.shape
    for i in range(0, n, 2):
        w = jnp.concatenate([w_ref[i], w_ref[i + 1]], 1)
        got = jnp.dot(a, w, preferred_element_type=F32).astype(BF16)
        out_ref[:, :, i * width : (i + 2) * width] = got.reshape(groups, per, 2 * width)


def qkv_body(loc_dev, head_dim, pos, own_ref, y1_ref, y2_ref, y3_ref, w_ref, keep_ref, send_ref, scratch):
    c, y, xh = pos[0], pos[3], pos[4]
    for k, ref in enumerate((own_ref, y1_ref, y2_ref, y3_ref)):
        slot = 2 * lax.rem(y - k + 4, 4)
        scratch[slot + xh] = ref[0]
        scratch[slot + 1 - xh] = ref[1]
    _, per, model = scratch.shape
    scratch[8] = jnp.ones((per, model), BF16)
    a = scratch[...].reshape(9 * per, model)
    rows = 8 * per
    got = jnp.dot(a, w_ref[...], preferred_element_type=F32)
    columns = w_ref.shape[1] // 3
    a_f = a[:rows].astype(F32)
    mean = jnp.mean(a_f, axis=1, keepdims=True)
    dev = a_f - mean
    spread = jnp.sum(dev * dev, axis=1, keepdims=True)
    at = lane((rows, LANES))
    wide = jnp.where(at == 0, mean, jnp.where(at == 1, spread, jnp.where(at == 2, mean * mean, 0.0)))
    stats = jnp.transpose(wide)
    base = 2 * rows + 4 * Q_DEV

    def write(ref, x, h):
        for i in (0, 1):
            ref[x, i * rows : (i + 1) * rows, :] = got[:rows, i * columns + h * head_dim : i * columns + (h + 1) * head_dim]
        lo = 2 * columns + h * head_dim
        for w in range(4):
            ref[x, 2 * rows + w * Q_DEV : 2 * rows + (w + 1) * Q_DEV, :] = got[w * loc_dev : w * loc_dev + Q_DEV, lo : lo + head_dim]
        for i in range(3):
            lo = i * columns + h * head_dim
            ref[x, base + i : base + i + 1, :] = got[rows : rows + 1, lo : lo + head_dim]
        ref[x, base + 3 : base + 8, :] = stats[:5]

    for x in (0, 1):
        for core in (0, 1):
            @pl.when(c == core)
            def _():
                write(keep_ref, x, 2 * x + core)

            @pl.when(c != core)
            def _():
                write(send_ref, x, 2 * x + core)


def shift(x, axis, by):
    n = lax.axis_size(axis)
    return lax.ppermute(x, axis, [(i, (i + by) % n) for i in range(n)])


def ring_gather(x, axis, split):
    n = lax.axis_size(axis)
    got = [(0, x)]
    up = down = x
    for k in range(1, n // 2):
        up, down = shift(up, axis, 1), shift(down, axis, -1)
        got += [(n - k, up), (k, down)]
    half = x.shape[split] // 2
    first, second = jnp.split(up, [half], split)[0], jnp.split(down, [half], split)[1]
    got.append((n // 2, jnp.concatenate([shift(first, axis, 1), shift(second, axis, -1)], split)))
    return got


def by_bit(bit, mine, other):
    return jnp.where(bit == 0, jnp.stack([mine, other]), jnp.stack([other, mine]))


def pick(x, i):
    return lax.dynamic_index_in_dim(x, i, 0, keepdims=False)


def on_device(tokens, slab_index, agg_query, agg_key_w, agg_value_w, agg_out_w, norm_gain, query_w, key_w, value_w):
    model = tokens.shape[2]
    rows_w, columns = agg_key_w.shape
    head_dim = model // HEADS
    heads = columns // head_dim
    factor = 1.0 / math.sqrt(head_dim)
    n_z = lax.axis_size("z")
    locs = tokens.shape[1]
    loc_dev = locs // (4 * n_z)
    xl, z, c = lax.axis_index("xl"), lax.axis_index("z"), lax.axis_index("c")
    y, xh = lax.axis_index("y"), lax.axis_index("xh")
    wide = lax.axis_index(WIDE)
    toks = tokens.reshape(locs, model)
    zs = [lax.rem(z + k, n_z) for k in range(n_z)]
    pos = jnp.stack([c, xl, z, y, xh, wide, slab_index[0], *zs]).astype(jnp.int32)

    out_z = lax.all_gather(agg_out_w, "z", axis=0)
    packed = call(
        functools.partial(pack_body, heads, factor),
        pos,
        sds((rows_w + PARTS, columns), BF16),
        [full((1, columns)), full(agg_key_w.shape), full(agg_value_w.shape)],
        full((rows_w + PARTS, columns)),
        (agg_query.reshape(1, columns), agg_key_w, agg_value_w),
    )

    pair = by_bit(xl, packed, shift(packed, "xl", 1))
    gathered = [(7 + k, b, shift(b, "c", 1)) for k, b in ring_gather(pair, "z", 2)]
    acc = value_call(pos, toks, gathered[:1], None, False, heads, loc_dev)
    for i in range(1, n_z - 1, 2):
        acc = value_call(pos, toks, gathered[i : i + 2], acc, False, heads, loc_dev)
    msg, v, s = value_call(pos, toks, gathered[n_z - 1 :], acc, True, heads, loc_dev)

    msg = shift(msg, "c", 1)
    half = locs // 4
    tile = half // 2
    ext = columns + LANES
    wide_spec = lambda w: pl.BlockSpec((2, tile, w), lambda i, s: (0, i, 0))
    row_spec = lambda w: pl.BlockSpec((tile, w), lambda i, s: (i, 0))
    msg, v, s = call(
        functools.partial(core_body, heads),
        pos,
        [sds((half, ext), BF16), sds((half, columns), F32), sds((half, LANES), F32)],
        [wide_spec(columns), wide_spec(LANES), wide_spec(ext)],
        [row_spec(ext), row_spec(columns), row_spec(LANES)],
        (v.reshape(2, half, columns), s.reshape(2, half, LANES), msg.reshape(2, half, ext)),
        grid=(2,),
    )
    msg = shift(msg, "xl", 1)
    msg = call(
        functools.partial(pair_body, heads),
        pos,
        sds((half, ext), BF16),
        [row_spec(columns), row_spec(LANES), row_spec(ext)],
        row_spec(ext),
        (v, s, msg),
        grid=(2,),
    )
    msg = lax.all_to_all(msg.reshape(n_z, loc_dev, ext), "z", 0, 0, tiled=True)
    agg = call(
        functools.partial(ring_body, heads),
        pos,
        sds((loc_dev, columns), BF16),
        [full(msg.shape)],
        full((loc_dev, columns)),
        (msg,),
        scratch=[pltpu.VMEM((2 * loc_dev, columns), F32)],
    )

    near = jnp.stack([agg, shift(agg, "c", 1)])
    far = shift(near, "xl", 1)
    n_rows = 4 * loc_dev
    n_head = lax.axis_size(HEAD)
    part = n_z * rows_w
    partial_sum = call(
        out_body,
        pos,
        sds((n_head, n_rows // n_head, part), BF16),
        [full(near.shape), full(far.shape), full(out_z.shape)],
        full((n_head, n_rows // n_head, part)),
        (near, far, out_z),
        scratch=[pltpu.VMEM((4, loc_dev, columns), BF16)],
        flops=2 * n_rows * columns * part,
    )
    got = lax.all_to_all(partial_sum, HEAD, 0, 0, tiled=True)
    mine = jnp.sum(got.astype(F32), axis=0).astype(BF16)
    two = jnp.stack([mine, shift(mine, "xh", 1)])
    others = [shift(two, "y", k) for k in (1, 2, 3)]

    gain = lax.dynamic_slice_in_dim(norm_gain, wide * rows_w, rows_w, 0)[:, None]
    scaled = jnp.concatenate([(gain * w.astype(F32)).astype(BF16) for w in (key_w, value_w, query_w)], 1)
    qkv_w = lax.all_gather(scaled, "z", axis=0, tiled=True)
    base = 2 * n_rows + 4 * Q_DEV
    sums_shape = (2, base + 8, head_dim)
    keep, send = call(
        functools.partial(qkv_body, loc_dev, head_dim),
        pos,
        [sds(sums_shape, F32)] * 2,
        [full(two.shape)] * 4 + [full(qkv_w.shape)],
        [full(sums_shape)] * 2,
        (two, *others, qkv_w),
        scratch=[pltpu.VMEM((n_head + 1, n_rows // n_head, part), BF16)],
        flops=2 * n_rows * part * 3 * columns,
    )
    sums = keep + shift(send, "c", 1)
    sums = pick(sums, xl) + shift(pick(sums, 1 - xl), "xl", 1)
    col = sums[base : base + 3]
    mean_all = sums[base + 3] / 4
    between = sums[base + 5] / 4 - mean_all * mean_all
    var = sums[base + 4] / model + jnp.maximum(between, 0.0)
    rstd = lax.rsqrt(var + 1e-05)

    def normed(x, i, m, r):
        return ((x - m[:, None] * col[i][None, :]) * r[:, None]).astype(BF16)

    slab_of = lambda x: x.reshape(4, loc_dev)[:, :Q_DEV].reshape(-1)
    key_out = normed(sums[:n_rows], 0, mean_all, rstd)
    value_out = normed(sums[n_rows : 2 * n_rows], 1, mean_all, rstd)
    query_out = normed(sums[2 * n_rows : base], 2, slab_of(mean_all), slab_of(rstd))

    kv_all = jnp.concatenate([b for _, b in ring_gather(jnp.concatenate([key_out, value_out], 1), "z", 0)], 0)
    scores = factor * lax.dot_general(
        query_out, kv_all[:, :head_dim], (((1,), (1,)), ((), ())), preferred_element_type=F32
    )
    probs = jax.nn.softmax(scores, axis=-1)
    attended = jnp.dot(probs, kv_all[:, head_dim:].astype(F32), precision=lax.Precision.HIGHEST)
    att = attended.astype(BF16).reshape(2, 2, Q_DEV, head_dim)
    att = jnp.moveaxis(att, 1, 0)
    att = by_bit(c, pick(att, c), shift(pick(att, 1 - c), "c", 1))
    att = jnp.moveaxis(att, 1, 0)
    att = by_bit(xl, pick(att, xl), shift(pick(att, 1 - xl), "xl", 1))
    return jnp.moveaxis(att.reshape(heads, Q_DEV, head_dim), 1, 0).reshape(Q_DEV, columns)


def solution(mesh):
    n_z = mesh.devices.shape[0] // 4
    fine = Mesh(mesh.devices.reshape(2, n_z, 2, 4, 2), WIDE + HEAD)
    placed = (
        P(WIDE, None, None),
        P(WIDE),
        P(HEAD),
        P(WIDE, HEAD),
        P(WIDE, HEAD),
        P(HEAD, WIDE),
        P(),
        P(WIDE, HEAD),
        P(WIDE, HEAD),
        P(WIDE, HEAD),
    )
    return jax.shard_map(on_device, mesh=fine, in_specs=placed, out_specs=P(WIDE, HEAD), check_vma=False)
```

time: 699 us -> 198 us (0.28)
  waiting for transfers between devices: 430 us -> 53.4 us
  local copies, waits for them, and re-layouts: 89.6 us -> 4.53 us
  other arithmetic: 54.6 us -> 3.07 us
  starting transfers between devices: 11.6 us -> 61.5 us
  matrix products: 45.9 us -> 0.65 us
  Pallas kernels: 0 us -> 28.6 us
  blocking collectives: 50.8 us -> 30.8 us
    all_gather x8 -> x2, waiting for transfers between devices: 229 us -> 0.01 us  [the longest x1 0.01 us: on_device(): out_z = lax.all_gather(agg_out_w, 'z', axis=0)]
    all_to_all x1 -> x0, waiting for transfers between devices: 198 us -> none  [on_device(): lax.all_to_all(tokens, 'wide', split_axis=1, concat_axis=0, tiled=True)]
    unnamed x14 -> x18, local copies, waits for them, and re-layouts: 83 us -> 3.17 us
    ppermute x0 -> x37, starting transfers between devices: none -> 61.4 us  [shift(): return lax.ppermute(x, axis, [(i, (i + by) % n) for i in range(n)])]
    unnamed x1 -> x0, other arithmetic: 53.6 us -> none
    ppermute x0 -> x37, waiting for transfers between devices: none -> 52.7 us  [shift(): return lax.ppermute(x, axis, [(i, (i + by) % n) for i in range(n)])]
    psum x1 -> x0, blocking collectives: 50.8 us -> none  [on_device(): aggregated = lax.psum(partial_sum, 'head').astype(jnp.bfloat16)]
    dot_general x10 -> x2, matrix products: 45.9 us -> 0.65 us  [the longest x1 0.34 us: on_device(): lax.dot_general(query_out, kv_all[:, :head_dim], (((1,), (1,)), ((), ()))...]
  transfers between devices with their start and end apart: 9 -> 39, of which waited for: 5 -> 21; matrix products, arithmetic and copies ran while one was open for 27% -> 2% of each run, Pallas kernels for 0% -> 14%
where the time goes in v1:
time: 198 us; the launch traced here: 197 us
  starting transfers between devices  61.5 us (31%)
  waiting for transfers between devices  53.4 us (27%)
  blocking collectives  30.8 us (16%)
  Pallas kernels  28.6 us (14%)
  between operations  14.4 us (7%)
  local copies, waits for them, and re-layouts  4.53 us (2%)
  other arithmetic  3.07 us (2%)
    ppermute x37, starting transfers between devices, shift(): return lax.ppermute(x, axis, [(i, (i + by) % n) for i in range(n)])  61.4 us
    ppermute x37, waiting for transfers between devices, shift(): return lax.ppermute(x, axis, [(i, (i + by) % n) for i in range(n)])  52.7 us
    pallas_call x11, Pallas kernels, call(): pl.pallas_call(body, out_shape=out_shape, grid_spec=pltpu.PrefetchScalarG...  28.6 us
    all_to_all x1, blocking collectives, on_device(): msg = lax.all_to_all(msg.reshape(n_z, loc_dev, ext), 'z', 0, 0, tiled=True)  16.1 us
    all_to_all x1, blocking collectives, on_device(): got = lax.all_to_all(partial_sum, HEAD, 0, 0, tiled=True)  14.6 us
  transfers between devices with their start and end apart: 39, of which 21 were waited for; matrix products, arithmetic and copies ran while one was open for 2% of the time, Pallas kernels for 14%

profile of v1, /device:TPU:1, one launch (start us, length us, event | category | flops | bytes accessed | tf_op | source)
XLA Modules:
  0.0 196.9 jit_solution(14020990245996193352)
XLA Ops:
  6.5 0.7 all-gather.6.cloned.1.call-update
  7.3 0.8 dynamic_slice.19
  8.1 1.2 multiply_convert_fusion.2
  9.3 0.8 pad_maximum_fusion
  10.9 0.7 shard_map.100
  11.6 2.1 %collective-permute-start = (bf16[144,512]{1,0:T(8,128)(2,1)S(1)}, bf16[144,512]{1,0:T(8,128)(2,1)S(1)}, u32[]{:S(2)}, u32[]{:S(2)}) collective-permute-start(bf16[144,512]{1,0:T(8,128)(2,1)S(1)} %shard_map.100), channel_id=1, source_target_pairs={{0,128},{128,0},{1,129},{129,1},{2,130},{130,2},{3,131},{131,3},{4... | collective-permute-start | bytes 442376 | tf_op jit(solution)/shard_map/ppermute | solution.py:275
  13.6 2.5 %collective-permute-done = bf16[144,512]{1,0:T(8,128)(2,1)S(1)} collective-permute-done((bf16[144,512]{1,0:T(8,128)(2,1)S(1)}, bf16[144,512]{1,0:T(8,128)(2,1)S(1)}, u32[]{:S(2)}, u32[]{:S(2)}) %collective-permute-start) | collective-permute-done | bytes 147488 | tf_op jit(solution)/shard_map/ppermute | solution.py:275
  16.2 2.7 %collective-permute-start.1 = (bf16[2,144,512]{2,1,0:T(8,128)(2,1)S(1)}, bf16[2,144,512]{2,1,0:T(8,128)(2,1)S(1)}, u32[]{:S(2)}, u32[]{:S(2)}) collective-permute-start(bf16[2,144,512]{2,1,0:T(8,128)(2,1)S(1)} %maximum_select_fusion.refs_4_), channel_id=1, source_target_pairs={{0,16},{16,32},{32,48},{48,64},{64,80},{80,96},{96,112},{112,0},{1... | collective-permute-start | bytes 884744 | tf_op jit(solution)/shard_map/ppermute | solution.py:275
  18.9 4.0 %collective-permute-start.5 = (bf16[2,144,512]{2,1,0:T(8,128)(2,1)S(1)}, bf16[2,144,512]{2,1,0:T(8,128)(2,1)S(1)}, u32[]{:S(2)}, u32[]{:S(2)}) collective-permute-start(bf16[2,144,512]{2,1,0:T(8,128)(2,1)S(1)} %maximum_select_fusion.refs_4_), channel_id=1, source_target_pairs={{0,112},{16,0},{32,16},{48,32},{64,48},{80,64},{96,80},{112,96},{1... | collective-permute-start | bytes 884744 | tf_op jit(solution)/shard_map/ppermute | solution.py:275
  22.9 6.1 %collective-permute-done.1.refs_8_ = bf16[2,144,512]{2,1,0:T(8,128)(2,1)S(1)} collective-permute-done((bf16[2,144,512]{2,1,0:T(8,128)(2,1)S(1)}, bf16[2,144,512]{2,1,0:T(8,128)(2,1)S(1)}, u32[]{:S(2)}, u32[]{:S(2)}) %collective-permute-start.1) | collective-permute-done | bytes 294944 | tf_op jit(solution)/shard_map/ppermute | solution.py:275
  29.0 1.1 collective-permute-done.5.refs_10_
  30.1 3.5 %collective-permute-start.6 = (bf16[2,144,512]{2,1,0:T(8,128)(2,1)S(1)}, bf16[2,144,512]{2,1,0:T(8,128)(2,1)S(1)}, u32[]{:S(2)}, u32[]{:S(2)}) collective-permute-start(bf16[2,144,512]{2,1,0:T(8,128)(2,1)S(1)} %collective-permute-done.5.refs_10_), channel_id=1, source_target_pairs={{0,112},{16,0},{32,16},{48,32},{64,48},{80,64},{96,80},{112,96},{1... | collective-permute-start | bytes 884744 | tf_op jit(solution)/shard_map/ppermute | solution.py:275
  33.6 5.8 %collective-permute-done.2.refs_8_ = bf16[2,144,512]{2,1,0:T(8,128)(2,1)S(1)} collective-permute-done((bf16[2,144,512]{2,1,0:T(8,128)(2,1)S(1)}, bf16[2,144,512]{2,1,0:T(8,128)(2,1)S(1)}, u32[]{:S(2)}, u32[]{:S(2)}) %collective-permute-start.2) | collective-permute-done | bytes 294944 | tf_op jit(solution)/shard_map/ppermute | solution.py:275
  39.4 1.8 collective-permute-done.6.refs_10_
  41.2 3.4 %collective-permute-start.7 = (bf16[2,144,512]{2,1,0:T(8,128)(2,1)S(1)}, bf16[2,144,512]{2,1,0:T(8,128)(2,1)S(1)}, u32[]{:S(2)}, u32[]{:S(2)}) collective-permute-start(bf16[2,144,512]{2,1,0:T(8,128)(2,1)S(1)} %collective-permute-done.6.refs_10_), channel_id=1, source_target_pairs={{0,112},{16,0},{32,16},{48,32},{64,48},{80,64},{96,80},{112,96},{1... | collective-permute-start | bytes 884744 | tf_op jit(solution)/shard_map/ppermute | solution.py:275
  44.7 4.0 %collective-permute-start.16 = (bf16[2,144,512]{2,1,0:T(8,128)(2,1)S(1)}, bf16[2,144,512]{2,1,0:T(8,128)(2,1)S(1)}, u32[]{:S(2)}, u32[]{:S(2)}) collective-permute-start(bf16[2,144,512]{2,1,0:T(8,128)(2,1)S(1)} %maximum_select_fusion.refs_4_), channel_id=1, source_target_pairs={{0,8},{8,0},{1,9},{9,1},{2,10},{10,2},{3,11},{11,3},{4,12},{12,4},... | collective-permute-start | bytes 884744 | tf_op jit(solution)/shard_map/ppermute | solution.py:275
  48.7 0.6 collective-permute-done.3.refs_8_
  49.4 4.4 %collective-permute-start.15 = (bf16[2,144,512]{2,1,0:T(8,128)(2,1)S(1)}, bf16[2,144,512]{2,1,0:T(8,128)(2,1)S(1)}, u32[]{:S(2)}, u32[]{:S(2)}) collective-permute-start(bf16[2,144,512]{2,1,0:T(8,128)(2,1)S(1)} %collective-permute-done.5.refs_10_), channel_id=1, source_target_pairs={{0,8},{8,0},{1,9},{9,1},{2,10},{10,2},{3,11},{11,3},{4,12},{12,4},... | collective-permute-start | bytes 884744 | tf_op jit(solution)/shard_map/ppermute | solution.py:275
  53.9 2.9 %collective-permute-start.8 = (bf16[2,144,256]{2,1,0:T(8,128)(2,1)S(1)}, bf16[2,144,256]{2,1,0:T(8,128)(2,1)S(1)}, u32[]{:S(2)}, u32[]{:S(2)}) collective-permute-start(bf16[2,144,256]{2,1,0:T(8,128)(2,1)S(1)} %split.17), channel_id=1, source_target_pairs={{0,112},{16,0},{32,16},{48,32},{64,48},{80,64},{96,80},{112,96},{1... | collective-permute-start | bytes 442376 | tf_op jit(solution)/shard_map/ppermute | solution.py:275
  56.8 3.7 %shard_map.101 = (f32[1024,512]{1,0:T(8,128)S(1)}, f32[1024,128]{1,0:T(8,128)S(1)}) custom-call(s32[15]{0:T(128)S(1)} %stack.115.pos, bf16[1024,4096]{1,0:T(8,128)(2,1)} %bitcast.77, bf16[1024,4096]{1,0:T(8,128)(2,1)} %bitcast.78, bf16[1024,4096]{1,0:T(8,128)(2,1)} %bitcast.79, bf16[1024,4096]{1,0:T(8,128)(2,1)} %bitcast.80, ...), custom_call_target="tpu_custom_call" | custom-call | flops 536870912 | bytes 36765696 | tf_op jit(solution)/shard_map/pallas_call | solution.py:26
  60.5 0.8 collective-permute-start.12
  61.4 0.5 collective-permute-start.10
  62.0 0.7 collective-permute-start.9
  62.7 4.7 %shard_map.102 = (f32[1024,512]{1,0:T(8,128)S(1)}, f32[1024,128]{1,0:T(8,128)S(1)}) custom-call(s32[15]{0:T(128)S(1)} %stack.115.pos, bf16[1024,4096]{1,0:T(8,128)(2,1)} %bitcast.81, bf16[1024,4096]{1,0:T(8,128)(2,1)} %bitcast.82, bf16[1024,4096]{1,0:T(8,128)(2,1)} %bitcast.83, ...), custom_call_target="tpu_custom_call", output_to_operand_aliasing={{0}: (13, {}), {1}: (14, {})} | custom-call | flops 1073741824 | bytes 73531392 | tf_op jit(solution)/shard_map/pallas_call | solution.py:26
  67.5 4.7 %shard_map.103 = (f32[1024,512]{1,0:T(8,128)S(1)}, f32[1024,128]{1,0:T(8,128)S(1)}) custom-call(s32[15]{0:T(128)S(1)} %stack.115.pos, bf16[1024,4096]{1,0:T(8,128)(2,1)} %bitcast.92, bf16[1024,4096]{1,0:T(8,128)(2,1)} %bitcast.90, bf16[1024,4096]{1,0:T(8,128)(2,1)} %bitcast.91, ...), custom_call_target="tpu_custom_call", output_to_operand_aliasing={{0}: (13, {}), {1}: (14, {})} | custom-call | flops 1073741824 | bytes 73531392 | tf_op jit(solution)/shard_map/pallas_call | solution.py:26
  72.2 4.7 %shard_map.104 = (f32[1024,512]{1,0:T(8,128)S(1)}, f32[1024,128]{1,0:T(8,128)S(1)}) custom-call(s32[15]{0:T(128)S(1)} %stack.115.pos, bf16[1024,4096]{1,0:T(8,128)(2,1)} %bitcast.97, bf16[1024,4096]{1,0:T(8,128)(2,1)} %bitcast.98, bf16[1024,4096]{1,0:T(8,128)(2,1)} %bitcast.99, ...), custom_call_target="tpu_custom_call", output_to_operand_aliasing={{0}: (13, {}), {1}: (14, {})} | custom-call | flops 1073741824 | bytes 73531392 | tf_op jit(solution)/shard_map/pallas_call | solution.py:26
  76.9 3.7 %shard_map.105 = (bf16[16,32,640]{2,1,0:T(8,128)(2,1)S(1)}, f32[16,32,512]{2,1,0:T(8,128)S(1)}, f32[16,32,128]{2,1,0:T(8,128)S(1)}) custom-call(s32[15]{0:T(128)S(1)} %stack.115.pos, bf16[1024,4096]{1,0:T(8,128)(2,1)} %bitcast.105, bf16[1024,4096]{1,0:T(8,128)(2,1)} %bitcast.106, bf16[1024,4096]{1,0:T(8,128)(2,1)} %bitcast.107, ...), custom_call_target="tpu_custom_call" | custom-call | flops 536870912 | bytes 38731776 | tf_op jit(solution)/shard_map/pallas_call | solution.py:26
  80.7 2.0 %collective-permute-done.17 = bf16[16,32,640]{2,1,0:T(8,128)(2,1)S(1)} collective-permute-done((bf16[16,32,640]{2,1,0:T(8,128)(2,1)S(1)}, bf16[16,32,640]{2,1,0:T(8,128)(2,1)S(1)}, u32[]{:S(2)}, u32[]{:S(2)}) %collective-permute-start.17) | collective-permute-done | bytes 655392 | tf_op jit(solution)/shard_map/ppermute | solution.py:275
  82.8 2.1 %shard_map.106 = (bf16[256,640]{1,0:T(8,128)(2,1)S(1)}, f32[256,512]{1,0:T(8,128)S(1)}, f32[256,128]{1,0:T(8,128)S(1)}) custom-call(s32[15]{0:T(128)S(1)} %stack.115.pos, f32[2,256,512]{2,1,0:T(8,128)S(1)} %bitcast.72, f32[2,256,128]{2,1,0:T(8,128)S(1)} %bitcast.75, bf16[2,256,640]{2,1,0:T(8,128)(2,1)S(1)} %bitcast.73), custom_call_target="tpu_custom_call" | custom-call | bytes 2949120 | tf_op jit(solution)/shard_map/pallas_call | solution.py:26
  84.9 1.2 collective-permute-start.18
  86.0 8.2 %collective-permute-done.18.msg_ref = bf16[256,640]{1,0:T(8,128)(2,1)S(1)} collective-permute-done((bf16[256,640]{1,0:T(8,128)(2,1)S(1)}, bf16[256,640]{1,0:T(8,128)(2,1)S(1)}, u32[]{:S(2)}, u32[]{:S(2)}) %collective-permute-start.18) | collective-permute-done | bytes 327712 | tf_op jit(solution)/shard_map/ppermute | solution.py:275
  94.2 1.3 shard_map.107
  95.5 16.1 %all_to_all.10.msg_ref = bf16[8,32,640]{2,1,0:T(8,128)(2,1)S(1)} all-to-all(bf16[8,32,640]{2,1,0:T(8,128)(2,1)S(1)} %bitcast.70), channel_id=1, replica_groups=mesh['xl'=2,'z'=8,'c'=2,'y'=4,'xh'=2] {'z'}, dimensions={0} | all-to-all | bytes 655360 | tf_op jit(solution)/shard_map/all_to_all | solution.py:357
  111.6 0.9 shard_map.108
  112.6 3.2 %collective-permute-start.19 = (bf16[32,512]{1,0:T(8,128)(2,1)S(1)}, bf16[32,512]{1,0:T(8,128)(2,1)S(1)}, u32[]{:S(2)}, u32[]{:S(2)}) collective-permute-start(bf16[32,512]{1,0:T(8,128)(2,1)S(1)} %shard_map.108), channel_id=1, source_target_pairs={{0,8},{8,0},{1,9},{9,1},{2,10},{10,2},{3,11},{11,3},{4,12},{12,4},... | collective-permute-start | bytes 98312 | tf_op jit(solution)/shard_map/ppermute | solution.py:275
  115.7 0.9 collective-permute-done.19
  116.6 1.4 collective-permute-start.20
  118.0 1.7 collective-permute-done.20.far_ref
  119.7 1.2 copy-done.1
  121.0 0.9 shard_map.109
  121.8 14.6 %all_to_all.11 = bf16[8,16,1024]{2,1,0:T(8,128)(2,1)S(1)} all-to-all(bf16[8,16,1024]{2,1,0:T(8,128)(2,1)S(1)} %shard_map.109), channel_id=1, replica_groups=mesh['xl'=2,'z'=8,'c'=2,'y'=4,'xh'=2] {'y','xh'}, dimensions={0} | all-to-all | bytes 524288 | tf_op jit(solution)/shard_map/all_to_all | solution.py:383
  136.5 0.5 collective-permute-start.21
  137.0 3.8 %collective-permute-done.21 = bf16[16,1024]{1,0:T(8,128)(2,1)S(1)} collective-permute-done((bf16[16,1024]{1,0:T(8,128)(2,1)S(1)}, bf16[16,1024]{1,0:T(8,128)(2,1)S(1)}, u32[]{:S(2)}, u32[]{:S(2)}) %collective-permute-start.21) | collective-permute-done | bytes 32800 | tf_op jit(solution)/shard_map/ppermute | solution.py:275
  141.0 1.6 collective-permute-start.23
  142.6 1.2 collective-permute-start.24
  143.8 2.2 %collective-permute-done.22.y1_ref = bf16[2,16,1024]{2,1,0:T(8,128)(2,1)S(1)} collective-permute-done((bf16[2,16,1024]{2,1,0:T(8,128)(2,1)S(1)}, bf16[2,16,1024]{2,1,0:T(8,128)(2,1)S(1)}, u32[]{:S(2)}, u32[]{:S(2)}) %collective-permute-start.22) | collective-permute-done | bytes 65568 | tf_op jit(solution)/shard_map/ppermute | solution.py:275
  146.0 0.6 collective-permute-done.24.y3_ref
  146.6 1.9 copy-done
  148.5 1.3 shard_map.110
  149.8 5.5 %collective-permute-start.25 = (f32[2,296,128]{2,1,0:T(8,128)S(1)}, f32[2,296,128]{2,1,0:T(8,128)S(1)}, u32[]{:S(2)}, u32[]{:S(2)}) collective-permute-start(f32[2,296,128]{2,1,0:T(8,128)S(1)} %get-tuple-element.36), channel_id=1, source_target_pairs={{0,8},{8,0},{1,9},{9,1},{2,10},{10,2},{3,11},{11,3},{4,12},{12,4},... | collective-permute-start | bytes 909320 | tf_op jit(solution)/shard_map/ppermute | solution.py:275
  155.2 1.2 collective-permute-done.25
  156.8 4.9 %collective-permute-done.26 = f32[296,128]{1,0:T(8,128)S(1)} collective-permute-done((f32[296,128]{1,0:T(8,128)S(1)}, f32[296,128]{1,0:T(8,128)S(1)}, u32[]{:S(2)}, u32[]{:S(2)}) %collective-permute-start.26) | collective-permute-done | bytes 151584 | tf_op jit(solution)/shard_map/ppermute | solution.py:275
  162.3 2.4 %collective-permute-start.28 = (bf16[128,256]{1,0:T(8,128)(2,1)S(1)}, bf16[128,256]{1,0:T(8,128)(2,1)S(1)}, u32[]{:S(2)}, u32[]{:S(2)}) collective-permute-start(bf16[128,256]{1,0:T(8,128)(2,1)S(1)} %get-tuple-element.49), channel_id=1, source_target_pairs={{0,112},{16,0},{32,16},{48,32},{64,48},{80,64},{96,80},{112,96},{1... | collective-permute-start | bytes 196616 | tf_op jit(solution)/shard_map/ppermute | solution.py:275
  165.1 1.2 collective-permute-done.27
  166.4 2.7 %collective-permute-start.30 = (bf16[128,256]{1,0:T(8,128)(2,1)S(1)}, bf16[128,256]{1,0:T(8,128)(2,1)S(1)}, u32[]{:S(2)}, u32[]{:S(2)}) collective-permute-start(bf16[128,256]{1,0:T(8,128)(2,1)S(1)} %collective-permute-done.28), channel_id=1, source_target_pairs={{0,112},{16,0},{32,16},{48,32},{64,48},{80,64},{96,80},{112,96},{1... | collective-permute-start | bytes 196616 | tf_op jit(solution)/shard_map/ppermute | solution.py:275
  169.1 1.6 collective-permute-done.29
  170.7 2.7 %collective-permute-start.32 = (bf16[128,256]{1,0:T(8,128)(2,1)S(1)}, bf16[128,256]{1,0:T(8,128)(2,1)S(1)}, u32[]{:S(2)}, u32[]{:S(2)}) collective-permute-start(bf16[128,256]{1,0:T(8,128)(2,1)S(1)} %collective-permute-done.30), channel_id=1, source_target_pairs={{0,112},{16,0},{32,16},{48,32},{64,48},{80,64},{96,80},{112,96},{1... | collective-permute-start | bytes 196616 | tf_op jit(solution)/shard_map/ppermute | solution.py:275
  173.4 1.6 collective-permute-done.31
  175.0 2.7 %collective-permute-start.34 = (bf16[64,256]{1,0:T(8,128)(2,1)S(1)}, bf16[64,256]{1,0:T(8,128)(2,1)S(1)}, u32[]{:S(2)}, u32[]{:S(2)}) collective-permute-start(bf16[64,256]{1,0:T(8,128)(2,1)S(1)} %split.19), channel_id=1, source_target_pairs={{0,112},{16,0},{32,16},{48,32},{64,48},{80,64},{96,80},{112,96},{1... | collective-permute-start | bytes 98312 | tf_op jit(solution)/shard_map/ppermute | solution.py:275
  177.8 1.8 collective-permute-done.33
  180.4 5.7 %collective-permute-start.35 = (bf16[2,8,128]{2,1,0:T(8,128)(2,1)S(1)}, bf16[2,8,128]{2,1,0:T(8,128)(2,1)S(1)}, u32[]{:S(2)}, u32[]{:S(2)}) collective-permute-start(bf16[2,8,128]{2,1,0:T(8,128)(2,1)S(1)} %get-tuple-element.54), channel_id=1, source_target_pairs={{0,8},{8,0},{1,9},{9,1},{2,10},{10,2},{3,11},{11,3},{4,12},{12,4},... | collective-permute-start | bytes 12296 | tf_op jit(solution)/shard_map/ppermute | solution.py:275
  186.1 0.8 collective-permute-done.35
  187.3 2.2 %collective-permute-done.36 = bf16[2,8,128]{2,1,0:T(8,128)(2,1)S(1)} collective-permute-done((bf16[2,8,128]{2,1,0:T(8,128)(2,1)S(1)}, bf16[2,8,128]{2,1,0:T(8,128)(2,1)S(1)}, u32[]{:S(2)}, u32[]{:S(2)}) %collective-permute-start.36) | collective-permute-done | bytes 4128 | tf_op jit(solution)/shard_map/ppermute | solution.py:275
  189.5 0.6 maximum_select_fusion.2
  (82 shorter events, 3.6 us)
Async XLA Ops:
  6.5 4.2 %copy-start.4 = (bf16[512]{0:T(512)(128)(2,1)S(1)}, bf16[512]{0:T(512)(128)(2,1)}, u32[]{:S(2)}) copy-start(bf16[512]{0:T(512)(128)(2,1)} %param.12) | copy-start | bytes 3076
  6.5 4.3 %copy-start.2 = (bf16[128,512]{1,0:T(8,128)(2,1)S(1)}, bf16[128,512]{1,0:T(8,128)(2,1)}, u32[]{:S(2)}) copy-start(bf16[128,512]{1,0:T(8,128)(2,1)} %key_ref.1) | copy-start | bytes 393220
  6.5 4.3 %copy-start.3 = (bf16[128,512]{1,0:T(8,128)(2,1)S(1)}, bf16[128,512]{1,0:T(8,128)(2,1)}, u32[]{:S(2)}) copy-start(bf16[128,512]{1,0:T(8,128)(2,1)} %value_ref.1) | copy-start | bytes 393220
  6.5 111.5 %all-gather.6.cloned.1.call-start = ((), (), s32[]{:S(2)}) async-start(), calls=%async_computation.3 | async-start | bytes 1179648 | tf_op jit(solution)/shard_map/all_gather | solution.py:315
  7.3 139.3 %all-gather.4.cloned.1.call-start = ((), (), s32[]{:S(2)}) async-start(), calls=%async_computation.2 | async-start | bytes 3538944 | tf_op jit(solution)/shard_map/all_gather | solution.py:390
  11.6 4.6 %collective-permute-start = (bf16[144,512]{1,0:T(8,128)(2,1)S(1)}, bf16[144,512]{1,0:T(8,128)(2,1)S(1)}, u32[]{:S(2)}, u32[]{:S(2)}) collective-permute-start(bf16[144,512]{1,0:T(8,128)(2,1)S(1)} %shard_map.100), channel_id=1, source_target_pairs={{0,128},{128,0},{1,129},{129,1},{2,130},{130,2},{3,131},{131,3},{4... | collective-permute-start | bytes 442376 | tf_op jit(solution)/shard_map/ppermute | solution.py:275
  16.2 12.8 %collective-permute-start.1 = (bf16[2,144,512]{2,1,0:T(8,128)(2,1)S(1)}, bf16[2,144,512]{2,1,0:T(8,128)(2,1)S(1)}, u32[]{:S(2)}, u32[]{:S(2)}) collective-permute-start(bf16[2,144,512]{2,1,0:T(8,128)(2,1)S(1)} %maximum_select_fusion.refs_4_), channel_id=1, source_target_pairs={{0,16},{16,32},{32,48},{48,64},{64,80},{80,96},{96,112},{112,0},{1... | collective-permute-start | bytes 884744 | tf_op jit(solution)/shard_map/ppermute | solution.py:275
  18.9 11.2 %collective-permute-start.5 = (bf16[2,144,512]{2,1,0:T(8,128)(2,1)S(1)}, bf16[2,144,512]{2,1,0:T(8,128)(2,1)S(1)}, u32[]{:S(2)}, u32[]{:S(2)}) collective-permute-start(bf16[2,144,512]{2,1,0:T(8,128)(2,1)S(1)} %maximum_select_fusion.refs_4_), channel_id=1, source_target_pairs={{0,112},{16,0},{32,16},{48,32},{64,48},{80,64},{96,80},{112,96},{1... | collective-permute-start | bytes 884744 | tf_op jit(solution)/shard_map/ppermute | solution.py:275
  29.0 10.3 %collective-permute-start.2 = (bf16[2,144,512]{2,1,0:T(8,128)(2,1)S(1)}, bf16[2,144,512]{2,1,0:T(8,128)(2,1)S(1)}, u32[]{:S(2)}, u32[]{:S(2)}) collective-permute-start(bf16[2,144,512]{2,1,0:T(8,128)(2,1)S(1)} %collective-permute-done.1.refs_8_), channel_id=1, source_target_pairs={{0,16},{16,32},{32,48},{48,64},{64,80},{80,96},{96,112},{112,0},{1... | collective-permute-start | bytes 884744 | tf_op jit(solution)/shard_map/ppermute | solution.py:275
  30.1 11.2 %collective-permute-start.6 = (bf16[2,144,512]{2,1,0:T(8,128)(2,1)S(1)}, bf16[2,144,512]{2,1,0:T(8,128)(2,1)S(1)}, u32[]{:S(2)}, u32[]{:S(2)}) collective-permute-start(bf16[2,144,512]{2,1,0:T(8,128)(2,1)S(1)} %collective-permute-done.5.refs_10_), channel_id=1, source_target_pairs={{0,112},{16,0},{32,16},{48,32},{64,48},{80,64},{96,80},{112,96},{1... | collective-permute-start | bytes 884744 | tf_op jit(solution)/shard_map/ppermute | solution.py:275
  39.3 10.0 %collective-permute-start.3 = (bf16[2,144,512]{2,1,0:T(8,128)(2,1)S(1)}, bf16[2,144,512]{2,1,0:T(8,128)(2,1)S(1)}, u32[]{:S(2)}, u32[]{:S(2)}) collective-permute-start(bf16[2,144,512]{2,1,0:T(8,128)(2,1)S(1)} %collective-permute-done.2.refs_8_), channel_id=1, source_target_pairs={{0,16},{16,32},{32,48},{48,64},{64,80},{80,96},{96,112},{112,0},{1... | collective-permute-start | bytes 884744 | tf_op jit(solution)/shard_map/ppermute | solution.py:275
  41.2 12.6 %collective-permute-start.7 = (bf16[2,144,512]{2,1,0:T(8,128)(2,1)S(1)}, bf16[2,144,512]{2,1,0:T(8,128)(2,1)S(1)}, u32[]{:S(2)}, u32[]{:S(2)}) collective-permute-start(bf16[2,144,512]{2,1,0:T(8,128)(2,1)S(1)} %collective-permute-done.6.refs_10_), channel_id=1, source_target_pairs={{0,112},{16,0},{32,16},{48,32},{64,48},{80,64},{96,80},{112,96},{1... | collective-permute-start | bytes 884744 | tf_op jit(solution)/shard_map/ppermute | solution.py:275
  44.7 12.1 %collective-permute-start.16 = (bf16[2,144,512]{2,1,0:T(8,128)(2,1)S(1)}, bf16[2,144,512]{2,1,0:T(8,128)(2,1)S(1)}, u32[]{:S(2)}, u32[]{:S(2)}) collective-permute-start(bf16[2,144,512]{2,1,0:T(8,128)(2,1)S(1)} %maximum_select_fusion.refs_4_), channel_id=1, source_target_pairs={{0,8},{8,0},{1,9},{9,1},{2,10},{10,2},{3,11},{11,3},{4,12},{12,4},... | collective-permute-start | bytes 884744 | tf_op jit(solution)/shard_map/ppermute | solution.py:275
  48.7 12.7 %collective-permute-start.14 = (bf16[2,144,512]{2,1,0:T(8,128)(2,1)S(1)}, bf16[2,144,512]{2,1,0:T(8,128)(2,1)S(1)}, u32[]{:S(2)}, u32[]{:S(2)}) collective-permute-start(bf16[2,144,512]{2,1,0:T(8,128)(2,1)S(1)} %collective-permute-done.1.refs_8_), channel_id=1, source_target_pairs={{0,8},{8,0},{1,9},{9,1},{2,10},{10,2},{3,11},{11,3},{4,12},{12,4},... | collective-permute-start | bytes 884744 | tf_op jit(solution)/shard_map/ppermute | solution.py:275
  49.4 11.9 %collective-permute-start.4 = (bf16[2,144,256]{2,1,0:T(8,128)(2,1)S(1)}, bf16[2,144,256]{2,1,0:T(8,128)(2,1)S(1)}, u32[]{:S(2)}, u32[]{:S(2)}) collective-permute-start(bf16[2,144,256]{2,1,0:T(8,128)(2,1)S(1)} %split.16), channel_id=1, source_target_pairs={{0,16},{16,32},{32,48},{48,64},{64,80},{80,96},{96,112},{112,0},{1... | collective-permute-start | bytes 442376 | tf_op jit(solution)/shard_map/ppermute | solution.py:275
  49.4 12.6 %collective-permute-start.15 = (bf16[2,144,512]{2,1,0:T(8,128)(2,1)S(1)}, bf16[2,144,512]{2,1,0:T(8,128)(2,1)S(1)}, u32[]{:S(2)}, u32[]{:S(2)}) collective-permute-start(bf16[2,144,512]{2,1,0:T(8,128)(2,1)S(1)} %collective-permute-done.5.refs_10_), channel_id=1, source_target_pairs={{0,8},{8,0},{1,9},{9,1},{2,10},{10,2},{3,11},{11,3},{4,12},{12,4},... | collective-permute-start | bytes 884744 | tf_op jit(solution)/shard_map/ppermute | solution.py:275
  53.9 8.0 %collective-permute-start.8 = (bf16[2,144,256]{2,1,0:T(8,128)(2,1)S(1)}, bf16[2,144,256]{2,1,0:T(8,128)(2,1)S(1)}, u32[]{:S(2)}, u32[]{:S(2)}) collective-permute-start(bf16[2,144,256]{2,1,0:T(8,128)(2,1)S(1)} %split.17), channel_id=1, source_target_pairs={{0,112},{16,0},{32,16},{48,32},{64,48},{80,64},{96,80},{112,96},{1... | collective-permute-start | bytes 442376 | tf_op jit(solution)/shard_map/ppermute | solution.py:275
  60.5 6.9 %collective-permute-start.12 = (bf16[2,144,512]{2,1,0:T(8,128)(2,1)S(1)}, bf16[2,144,512]{2,1,0:T(8,128)(2,1)S(1)}, u32[]{:S(2)}, u32[]{:S(2)}) collective-permute-start(bf16[2,144,512]{2,1,0:T(8,128)(2,1)S(1)} %collective-permute-done.2.refs_8_), channel_id=1, source_target_pairs={{0,8},{8,0},{1,9},{9,1},{2,10},{10,2},{3,11},{11,3},{4,12},{12,4},... | collective-permute-start | bytes 884744 | tf_op jit(solution)/shard_map/ppermute | solution.py:275
  61.3 6.2 %collective-permute-start.13 = (bf16[2,144,512]{2,1,0:T(8,128)(2,1)S(1)}, bf16[2,144,512]{2,1,0:T(8,128)(2,1)S(1)}, u32[]{:S(2)}, u32[]{:S(2)}) collective-permute-start(bf16[2,144,512]{2,1,0:T(8,128)(2,1)S(1)} %collective-permute-done.6.refs_10_), channel_id=1, source_target_pairs={{0,8},{8,0},{1,9},{9,1},{2,10},{10,2},{3,11},{11,3},{4,12},{12,4},... | collective-permute-start | bytes 884744 | tf_op jit(solution)/shard_map/ppermute | solution.py:275
  61.4 10.8 %collective-permute-start.10 = (bf16[2,144,512]{2,1,0:T(8,128)(2,1)S(1)}, bf16[2,144,512]{2,1,0:T(8,128)(2,1)S(1)}, u32[]{:S(2)}, u32[]{:S(2)}) collective-permute-start(bf16[2,144,512]{2,1,0:T(8,128)(2,1)S(1)} %collective-permute-done.3.refs_8_), channel_id=1, source_target_pairs={{0,8},{8,0},{1,9},{9,1},{2,10},{10,2},{3,11},{11,3},{4,12},{12,4},... | collective-permute-start | bytes 884744 | tf_op jit(solution)/shard_map/ppermute | solution.py:275
  61.9 10.3 %collective-permute-start.11 = (bf16[2,144,512]{2,1,0:T(8,128)(2,1)S(1)}, bf16[2,144,512]{2,1,0:T(8,128)(2,1)S(1)}, u32[]{:S(2)}, u32[]{:S(2)}) collective-permute-start(bf16[2,144,512]{2,1,0:T(8,128)(2,1)S(1)} %collective-permute-done.7.refs_10_), channel_id=1, source_target_pairs={{0,8},{8,0},{1,9},{9,1},{2,10},{10,2},{3,11},{11,3},{4,12},{12,4},... | collective-permute-start | bytes 884744 | tf_op jit(solution)/shard_map/ppermute | solution.py:275
  62.0 14.8 %collective-permute-start.9 = (bf16[2,144,512]{2,1,0:T(8,128)(2,1)S(1)}, bf16[2,144,512]{2,1,0:T(8,128)(2,1)S(1)}, u32[]{:S(2)}, u32[]{:S(2)}) collective-permute-start(bf16[2,144,512]{2,1,0:T(8,128)(2,1)S(1)} %constant_dynamic-update-slice_fusion.refs_4_), channel_id=1, source_target_pairs={{0,8},{8,0},{1,9},{9,1},{2,10},{10,2},{3,11},{11,3},{4,12},{12,4},... | collective-permute-start | bytes 884744 | tf_op jit(solution)/shard_map/ppermute | solution.py:275
  80.6 2.2 %collective-permute-start.17 = (bf16[16,32,640]{2,1,0:T(8,128)(2,1)S(1)}, bf16[16,32,640]{2,1,0:T(8,128)(2,1)S(1)}, u32[]{:S(2)}, u32[]{:S(2)}) collective-permute-start(bf16[16,32,640]{2,1,0:T(8,128)(2,1)S(1)} %get-tuple-element.31), channel_id=1, source_target_pairs={{0,8},{8,0},{1,9},{9,1},{2,10},{10,2},{3,11},{11,3},{4,12},{12,4},... | collective-permute-start | bytes 1966088 | tf_op jit(solution)/shard_map/ppermute | solution.py:275
  84.9 9.4 %collective-permute-start.18 = (bf16[256,640]{1,0:T(8,128)(2,1)S(1)}, bf16[256,640]{1,0:T(8,128)(2,1)S(1)}, u32[]{:S(2)}, u32[]{:S(2)}) collective-permute-start(bf16[256,640]{1,0:T(8,128)(2,1)S(1)} %get-tuple-element.34), channel_id=1, source_target_pairs={{0,128},{128,0},{1,129},{129,1},{2,130},{130,2},{3,131},{131,3},{4... | collective-permute-start | bytes 983048 | tf_op jit(solution)/shard_map/ppermute | solution.py:275
  112.6 4.0 %collective-permute-start.19 = (bf16[32,512]{1,0:T(8,128)(2,1)S(1)}, bf16[32,512]{1,0:T(8,128)(2,1)S(1)}, u32[]{:S(2)}, u32[]{:S(2)}) collective-permute-start(bf16[32,512]{1,0:T(8,128)(2,1)S(1)} %shard_map.108), channel_id=1, source_target_pairs={{0,8},{8,0},{1,9},{9,1},{2,10},{10,2},{3,11},{11,3},{4,12},{12,4},... | collective-permute-start | bytes 98312 | tf_op jit(solution)/shard_map/ppermute | solution.py:275
  116.6 3.2 %collective-permute-start.20 = (bf16[2,32,512]{2,1,0:T(8,128)(2,1)S(1)}, bf16[2,32,512]{2,1,0:T(8,128)(2,1)S(1)}, u32[]{:S(2)}, u32[]{:S(2)}) collective-permute-start(bf16[2,32,512]{2,1,0:T(8,128)(2,1)S(1)} %pad_maximum_fusion.1.own_ref), channel_id=1, source_target_pairs={{0,128},{128,0},{1,129},{129,1},{2,130},{130,2},{3,131},{131,3},{4... | collective-permute-start | bytes 196616 | tf_op jit(solution)/shard_map/ppermute | solution.py:275
  119.7 1.2 copy-start.1
  136.5 4.4 %collective-permute-start.21 = (bf16[16,1024]{1,0:T(8,128)(2,1)S(1)}, bf16[16,1024]{1,0:T(8,128)(2,1)S(1)}, u32[]{:S(2)}, u32[]{:S(2)}) collective-permute-start(bf16[16,1024]{1,0:T(8,128)(2,1)S(1)} %reduce_sum.21), channel_id=1, source_target_pairs={{0,1},{1,0},{2,3},{3,2},{4,5},{5,4},{6,7},{7,6},{8,9},{9,8},{10,11... | collective-permute-start | bytes 98312 | tf_op jit(solution)/shard_map/ppermute | solution.py:275
  140.9 5.1 %collective-permute-start.22 = (bf16[2,16,1024]{2,1,0:T(8,128)(2,1)S(1)}, bf16[2,16,1024]{2,1,0:T(8,128)(2,1)S(1)}, u32[]{:S(2)}, u32[]{:S(2)}) collective-permute-start(bf16[2,16,1024]{2,1,0:T(8,128)(2,1)S(1)} %pad_maximum_fusion.2.own_ref), channel_id=1, source_target_pairs={{0,2},{2,4},{4,6},{6,0},{1,3},{3,5},{5,7},{7,1},{8,10},{10,12},{12... | collective-permute-start | bytes 196616 | tf_op jit(solution)/shard_map/ppermute | solution.py:275
  141.0 5.0 %collective-permute-start.23 = (bf16[2,16,1024]{2,1,0:T(8,128)(2,1)S(1)}, bf16[2,16,1024]{2,1,0:T(8,128)(2,1)S(1)}, u32[]{:S(2)}, u32[]{:S(2)}) collective-permute-start(bf16[2,16,1024]{2,1,0:T(8,128)(2,1)S(1)} %pad_maximum_fusion.2.own_ref), channel_id=1, source_target_pairs={{0,4},{2,6},{4,0},{6,2},{1,5},{3,7},{5,1},{7,3},{8,12},{10,14},{12... | collective-permute-start | bytes 196616 | tf_op jit(solution)/shard_map/ppermute | solution.py:275
  142.6 4.0 %collective-permute-start.24 = (bf16[2,16,1024]{2,1,0:T(8,128)(2,1)S(1)}, bf16[2,16,1024]{2,1,0:T(8,128)(2,1)S(1)}, u32[]{:S(2)}, u32[]{:S(2)}) collective-permute-start(bf16[2,16,1024]{2,1,0:T(8,128)(2,1)S(1)} %pad_maximum_fusion.2.own_ref), channel_id=1, source_target_pairs={{0,6},{2,0},{4,2},{6,4},{1,7},{3,1},{5,3},{7,5},{8,14},{10,8},{12,... | collective-permute-start | bytes 196616 | tf_op jit(solution)/shard_map/ppermute | solution.py:275
  146.6 1.9 copy-start
  149.8 6.7 %collective-permute-start.25 = (f32[2,296,128]{2,1,0:T(8,128)S(1)}, f32[2,296,128]{2,1,0:T(8,128)S(1)}, u32[]{:S(2)}, u32[]{:S(2)}) collective-permute-start(f32[2,296,128]{2,1,0:T(8,128)S(1)} %get-tuple-element.36), channel_id=1, source_target_pairs={{0,8},{8,0},{1,9},{9,1},{2,10},{10,2},{3,11},{11,3},{4,12},{12,4},... | collective-permute-start | bytes 909320 | tf_op jit(solution)/shard_map/ppermute | solution.py:275
  156.5 5.2 %collective-permute-start.26 = (f32[296,128]{1,0:T(8,128)S(1)}, f32[296,128]{1,0:T(8,128)S(1)}, u32[]{:S(2)}, u32[]{:S(2)}) collective-permute-start(f32[296,128]{1,0:T(8,128)S(1)} %dynamic-slice_bitcast_fusion), channel_id=1, source_target_pairs={{0,128},{128,0},{1,129},{129,1},{2,130},{130,2},{3,131},{131,3},{4... | collective-permute-start | bytes 454664 | tf_op jit(solution)/shard_map/ppermute | solution.py:275
  161.9 4.4 %collective-permute-start.27 = (bf16[128,256]{1,0:T(8,128)(2,1)S(1)}, bf16[128,256]{1,0:T(8,128)(2,1)S(1)}, u32[]{:S(2)}, u32[]{:S(2)}) collective-permute-start(bf16[128,256]{1,0:T(8,128)(2,1)S(1)} %get-tuple-element.49), channel_id=1, source_target_pairs={{0,16},{16,32},{32,48},{48,64},{64,80},{80,96},{96,112},{112,0},{1... | collective-permute-start | bytes 196616 | tf_op jit(solution)/shard_map/ppermute | solution.py:275
  162.3 4.1 %collective-permute-start.28 = (bf16[128,256]{1,0:T(8,128)(2,1)S(1)}, bf16[128,256]{1,0:T(8,128)(2,1)S(1)}, u32[]{:S(2)}, u32[]{:S(2)}) collective-permute-start(bf16[128,256]{1,0:T(8,128)(2,1)S(1)} %get-tuple-element.49), channel_id=1, source_target_pairs={{0,112},{16,0},{32,16},{48,32},{64,48},{80,64},{96,80},{112,96},{1... | collective-permute-start | bytes 196616 | tf_op jit(solution)/shard_map/ppermute | solution.py:275
  166.3 4.3 %collective-permute-start.29 = (bf16[128,256]{1,0:T(8,128)(2,1)S(1)}, bf16[128,256]{1,0:T(8,128)(2,1)S(1)}, u32[]{:S(2)}, u32[]{:S(2)}) collective-permute-start(bf16[128,256]{1,0:T(8,128)(2,1)S(1)} %collective-permute-done.27), channel_id=1, source_target_pairs={{0,16},{16,32},{32,48},{48,64},{64,80},{80,96},{96,112},{112,0},{1... | collective-permute-start | bytes 196616 | tf_op jit(solution)/shard_map/ppermute | solution.py:275
  166.4 4.3 %collective-permute-start.30 = (bf16[128,256]{1,0:T(8,128)(2,1)S(1)}, bf16[128,256]{1,0:T(8,128)(2,1)S(1)}, u32[]{:S(2)}, u32[]{:S(2)}) collective-permute-start(bf16[128,256]{1,0:T(8,128)(2,1)S(1)} %collective-permute-done.28), channel_id=1, source_target_pairs={{0,112},{16,0},{32,16},{48,32},{64,48},{80,64},{96,80},{112,96},{1... | collective-permute-start | bytes 196616 | tf_op jit(solution)/shard_map/ppermute | solution.py:275
  170.7 4.3 %collective-permute-start.31 = (bf16[128,256]{1,0:T(8,128)(2,1)S(1)}, bf16[128,256]{1,0:T(8,128)(2,1)S(1)}, u32[]{:S(2)}, u32[]{:S(2)}) collective-permute-start(bf16[128,256]{1,0:T(8,128)(2,1)S(1)} %collective-permute-done.29), channel_id=1, source_target_pairs={{0,16},{16,32},{32,48},{48,64},{64,80},{80,96},{96,112},{112,0},{1... | collective-permute-start | bytes 196616 | tf_op jit(solution)/shard_map/ppermute | solution.py:275
  170.7 4.3 %collective-permute-start.32 = (bf16[128,256]{1,0:T(8,128)(2,1)S(1)}, bf16[128,256]{1,0:T(8,128)(2,1)S(1)}, u32[]{:S(2)}, u32[]{:S(2)}) collective-permute-start(bf16[128,256]{1,0:T(8,128)(2,1)S(1)} %collective-permute-done.30), channel_id=1, source_target_pairs={{0,112},{16,0},{32,16},{48,32},{64,48},{80,64},{96,80},{112,96},{1... | collective-permute-start | bytes 196616 | tf_op jit(solution)/shard_map/ppermute | solution.py:275
  175.0 4.5 %collective-permute-start.33 = (bf16[64,256]{1,0:T(8,128)(2,1)S(1)}, bf16[64,256]{1,0:T(8,128)(2,1)S(1)}, u32[]{:S(2)}, u32[]{:S(2)}) collective-permute-start(bf16[64,256]{1,0:T(8,128)(2,1)S(1)} %split.18), channel_id=1, source_target_pairs={{0,16},{16,32},{32,48},{48,64},{64,80},{80,96},{96,112},{112,0},{1... | collective-permute-start | bytes 98312 | tf_op jit(solution)/shard_map/ppermute | solution.py:275
  175.0 4.5 %collective-permute-start.34 = (bf16[64,256]{1,0:T(8,128)(2,1)S(1)}, bf16[64,256]{1,0:T(8,128)(2,1)S(1)}, u32[]{:S(2)}, u32[]{:S(2)}) collective-permute-start(bf16[64,256]{1,0:T(8,128)(2,1)S(1)} %split.19), channel_id=1, source_target_pairs={{0,112},{16,0},{32,16},{48,32},{64,48},{80,64},{96,80},{112,96},{1... | collective-permute-start | bytes 98312 | tf_op jit(solution)/shard_map/ppermute | solution.py:275
  180.4 6.5 %collective-permute-start.35 = (bf16[2,8,128]{2,1,0:T(8,128)(2,1)S(1)}, bf16[2,8,128]{2,1,0:T(8,128)(2,1)S(1)}, u32[]{:S(2)}, u32[]{:S(2)}) collective-permute-start(bf16[2,8,128]{2,1,0:T(8,128)(2,1)S(1)} %get-tuple-element.54), channel_id=1, source_target_pairs={{0,8},{8,0},{1,9},{9,1},{2,10},{10,2},{3,11},{11,3},{4,12},{12,4},... | collective-permute-start | bytes 12296 | tf_op jit(solution)/shard_map/ppermute | solution.py:275
  186.9 2.5 %collective-permute-start.36 = (bf16[2,8,128]{2,1,0:T(8,128)(2,1)S(1)}, bf16[2,8,128]{2,1,0:T(8,128)(2,1)S(1)}, u32[]{:S(2)}, u32[]{:S(2)}) collective-permute-start(bf16[2,8,128]{2,1,0:T(8,128)(2,1)S(1)} %get-tuple-element.52), channel_id=1, source_target_pairs={{0,128},{128,0},{1,129},{129,1},{2,130},{130,2},{3,131},{131,3},{4... | collective-permute-start | bytes 12296 | tf_op jit(solution)/shard_map/ppermute | solution.py:275
Sparse Core Ops, SparseCore 0:
  9.2 41.1 all-gather.5
  52.1 46.7 all-gather.3

commit v2 on v1

v2 whole, which is shorter than its diff:
```python
import functools
import math

import jax
import jax.numpy as jnp
from jax import lax
from jax.experimental import pallas as pl
from jax.experimental.pallas import tpu as pltpu
from jax.sharding import Mesh, PartitionSpec as P

HEADS = 32
Q_DEV = 8
F32 = jnp.float32
BF16 = jnp.bfloat16
WIDE = ("xl", "z", "c")
HEAD = ("y", "xh")
LANES = 128
PARTS = 16
NT = (((1,), (1,)), ((), ()))
VMEM_BYTES = 44 * 1024 * 1024


def call(body, pos, out_shape, in_specs, out_specs, args, grid=(1,), scratch=(), cost=1, after=()):
    n_in, n_after = len(in_specs), len(after)
    kernel = body
    if n_after:
        kernel = lambda pos, *refs: body(pos, *refs[:n_in], *refs[n_in + n_after :])
    in_specs = list(in_specs) + [pl.BlockSpec(memory_space=pl.ANY)] * n_after
    return pl.pallas_call(
        kernel,
        out_shape=out_shape,
        grid_spec=pltpu.PrefetchScalarGridSpec(
            num_scalar_prefetch=1, grid=grid, in_specs=in_specs, out_specs=out_specs, scratch_shapes=list(scratch)
        ),
        compiler_params=pltpu.CompilerParams(vmem_limit_bytes=VMEM_BYTES),
        cost_estimate=pl.CostEstimate(flops=cost, bytes_accessed=1, transcendentals=0),
    )(pos, *args, *after)


def full(shape):
    return pl.BlockSpec(shape, lambda i, s: (0,) * len(shape))


def sds(shape, dtype):
    return jax.ShapeDtypeStruct(shape, dtype)


def lane(shape):
    return lax.broadcasted_iota(jnp.int32, shape, len(shape) - 1)


def rounded(x):
    return x.astype(BF16).astype(F32)


def side_by_side(blocks):
    total = sum(b.shape[1] for b in blocks)
    col = lax.broadcasted_iota(jnp.int32, (blocks[0].shape[0], total), 1)
    out, start = None, 0
    for b in blocks:
        here = jnp.pad(b, ((0, 0), (start, total - start - b.shape[1])))
        out = here if out is None else jnp.where(col >= start, here, out)
        start += b.shape[1]
    return out


def same_body(*refs):
    pass


def once(x, after):
    anywhere = pl.BlockSpec(memory_space=pl.ANY)
    return pl.pallas_call(
        same_body,
        out_shape=sds(x.shape, x.dtype),
        in_specs=[anywhere] * 2,
        out_specs=anywhere,
        input_output_aliases={0: 0},
        cost_estimate=pl.CostEstimate(flops=1, bytes_accessed=1, transcendentals=0),
    )(x, after)


def split3(x):
    hi = lax.reduce_precision(x, 8, 7)
    mid = lax.reduce_precision(x - hi, 8, 7)
    low = lax.reduce_precision(x - hi - mid, 8, 7)
    return hi.astype(BF16), mid.astype(BF16), low.astype(BF16)


def fold(x, heads):
    total = x + pltpu.roll(x, LANES - heads, 1) + pltpu.roll(x, LANES - 2 * heads, 1)
    return jnp.where(lane(x.shape) < heads, total, 0.0)


def unfold(s, heads):
    s = jnp.where(lane(s.shape) < heads, s, 0.0)
    hi = rounded(s)
    mid = rounded(s - hi)
    low = s - hi - mid
    return (hi + pltpu.roll(mid, heads, 1) + pltpu.roll(low, 2 * heads, 1)).astype(BF16)


def pack_rows(s, heads):
    parts = unfold(s, heads).astype(F32)
    n = s.shape[0] // 4
    packed = parts[:n]
    for q in (1, 2, 3):
        packed = packed + pltpu.roll(parts[q * n : (q + 1) * n], q * LANES // 4, 1)
    return jnp.concatenate([packed[q * n // 4 : (q + 1) * n // 4] for q in range(4)], 1).astype(BF16)


def unpack_rows(rows, heads):
    rows = rows.astype(F32)
    packed = jnp.concatenate([rows[:, q * LANES : (q + 1) * LANES] for q in range(4)], 0)
    return jnp.concatenate([fold(packed if q == 0 else pltpu.roll(packed, LANES - q * LANES // 4, 1), heads) for q in range(4)], 0)


def widen(p, heads, head_dim):
    return jnp.concatenate([jnp.broadcast_to(p[:, h : h + 1], (p.shape[0], head_dim)) for h in range(heads)], 1)


def merge(v0, s0, v1, s1, heads, head_dim):
    top = jnp.maximum(s0, s1)
    e0, e1 = jnp.exp(s0 - top), jnp.exp(s1 - top)
    total = e0 + e1
    v = widen(e0 / total, heads, head_dim) * v0 + widen(e1 / total, heads, head_dim) * v1.astype(F32)
    return v, top + jnp.log(total)


def value_body(pieces, n_tok, n_blocks, first, last, heads, pos, *refs):
    toks = refs[:n_tok]
    blocks = refs[n_tok : n_tok + n_blocks]
    rest = refs[n_tok + n_blocks :]
    rows, d = toks[0].shape[0], toks[0].shape[1] // 2
    lhs, rhs, parts = [], [], []
    for tok, flip, block, place in pieces:
        core = pos[0] if flip == 0 else 1 - pos[0]
        lhs.append(toks[tok][:, pl.ds(pl.multiple_of(core * d, d), d)])
        rhs.append(blocks[block][place, :d, :])
        parts.append(blocks[block][place, d:, :d])
    lhs = jnp.concatenate(lhs, 1)
    v = jnp.dot(lhs, jnp.concatenate(rhs, 0), preferred_element_type=F32)
    s = lax.dot_general(lhs, jnp.concatenate(parts, 1), NT, preferred_element_type=F32)
    s = jnp.concatenate([s, jnp.zeros((rows, LANES - PARTS), F32)], 1)
    if not first:
        v = v + rest[0][...]
        s = s + rest[1][...]
        rest = rest[2:]
    if not last:
        rest[0][...] = v
        rest[1][...] = s
        return
    msg_ref, v_ref, s_ref = rest
    groups, loc_dev, width = v_ref.shape
    s = fold(s, heads)
    v4 = v.reshape(groups, 2, loc_dev, width)
    s4 = s.reshape(groups, 2, loc_dev, LANES)
    p4 = unfold(s, heads).astype(F32).reshape(groups, 2, loc_dev, LANES)
    even = pos[0] == 0
    v_ref[...] = jnp.where(even, v4[:, 0], v4[:, 1])
    s_ref[...] = jnp.where(even, s4[:, 0], s4[:, 1])
    msg_ref[:, :, :width] = jnp.where(even, v4[:, 1], v4[:, 0]).astype(BF16)
    msg_ref[:, :, width:] = jnp.where(even, p4[:, 1], p4[:, 0]).astype(BF16)


def value_call(pos, toks, chunks, acc, last, heads, loc_dev, mine, after=(), tile=512):
    locs, model = toks.shape[0] // 2, toks.shape[1]
    arrays, pieces, in_specs, args = [], [], [], []
    for offset, blocks in chunks:
        for x in (0, 1):
            def place(i, s, offset=offset, x=x):
                side = s[1] if x == 0 else 1 - s[1]
                half = s[1] if mine else 1 - s[1]
                return half * (locs // tile) + i, side * (model // 512) + s[7 + offset]
            in_specs.append(pl.BlockSpec((tile, 256), place))
            args.append(toks)
            for flip in (0, 1):
                array, at = blocks[x][flip]
                found = [i for i, o in enumerate(arrays) if o is array]
                if not found:
                    arrays.append(array)
                pieces.append((len(args) - 1, flip, found[0] if found else len(arrays) - 1, at))
    n_tok = len(args)
    in_specs += [full(o.shape) for o in arrays]
    args += arrays
    width = arrays[0].shape[2]
    rows2 = [pl.BlockSpec((tile, width), lambda i, s: (i, 0)), pl.BlockSpec((tile, LANES), lambda i, s: (i, 0))]
    if acc is not None:
        in_specs += rows2
        args += list(acc)
    if last:
        g = tile // (2 * loc_dev)
        total = locs // (2 * loc_dev)
        shapes = [(total, loc_dev, width + LANES), (total, loc_dev, width), (total, loc_dev, LANES)]
        out_shape = [sds(sh, t) for sh, t in zip(shapes, (BF16, F32, F32))]
        out_specs = [pl.BlockSpec((g,) + sh[1:], lambda i, s: (i, 0, 0)) for sh in shapes]
    else:
        out_shape = [sds((locs, width), F32), sds((locs, LANES), F32)]
        out_specs = rows2
    body = functools.partial(value_body, pieces, n_tok, len(arrays), acc is None, last, heads)
    return call(body, pos, out_shape, in_specs, out_specs, args, grid=(locs // tile,), after=after)


def stack_body(pos, *refs):
    for i, ref in enumerate(refs[:-1]):
        refs[-1][i] = ref[...]


def side_body(pos, left_ref, right_ref, out_ref):
    width = left_ref.shape[1]
    out_ref[0, :, :width] = left_ref[...]
    out_ref[0, :, width:] = right_ref[...]


def join_body(pos, *refs):
    start = 0
    for ref in refs[:-1]:
        refs[-1][start : start + ref.shape[0]] = ref[...]
        start += ref.shape[0]


def first_body(heads, pos, v_ref, s_ref, msg_ref, out_ref):
    rows, width = v_ref.shape
    s1 = fold(msg_ref[:, width:].astype(F32), heads)
    v, s = merge(v_ref[...], s_ref[...], msg_ref[:, :width], s1, heads, width // heads)
    out_ref[:rows, :] = v.astype(BF16)
    out_ref[rows:, :] = pack_rows(s, heads)


def last_body(heads, pos, v_ref, s_ref, far_ref, top_ref, bottom_ref, out_ref):
    width = v_ref.shape[-1]
    rows = v_ref.shape[0]
    near = jnp.concatenate([top_ref[...], bottom_ref[...]], 0)
    logs = [s_ref[...], unpack_rows(far_ref[rows:, :], heads), fold(near[:, width:].astype(F32), heads)]
    values = [v_ref[...], far_ref[:rows, :].astype(F32), near[:, :width].astype(F32)]
    top = functools.reduce(jnp.maximum, logs)
    powers = [jnp.exp(x - top) for x in logs]
    total = functools.reduce(jnp.add, powers)
    v = sum(widen(p / total, heads, width // heads) * x for p, x in zip(powers, values))
    out_ref[:, :width] = v.astype(BF16)
    out_ref[:, width:] = unfold(top + jnp.log(total), heads)


def pair_call(pos, v, s, msg, heads, to_send, after=()):
    rows, width = v.shape
    tile = rows // 2
    specs = [pl.BlockSpec((tile, w), lambda i, s: (i, 0)) for w in (width, LANES, width + LANES)]
    if to_send:
        out, out_specs = sds(msg.shape, BF16), specs[2]
    else:
        out, out_specs = [sds(v.shape, F32), sds(s.shape, F32)], specs[:2]
    return call(functools.partial(pair_body, heads), pos, out, specs, out_specs, (v, s, msg), grid=(2,), after=after)


def ring_body(heads, pos, msg_ref, out_ref, scratch):
    n, rows, width = msg_ref.shape
    width -= LANES
    logs = [fold(msg_ref[i, :, width:].astype(F32), heads) for i in range(n)]
    top = functools.reduce(jnp.maximum, logs)
    powers = [jnp.exp(s - top) for s in logs]
    total = functools.reduce(jnp.add, powers)
    out = jnp.zeros((rows, width), F32)
    for i in range(n):
        out += widen(powers[i] / total, heads, width // heads) * msg_ref[i, :, :width].astype(F32)
    scratch[:rows, :] = out
    scratch[rows:, :] = out
    start = pl.multiple_of(pos[6] * Q_DEV, Q_DEV)
    out_ref[...] = scratch[pl.ds(start, rows), :].astype(BF16)


def out_body(pos, own_ref, far_ref, w_ref, *refs):
    outs, scratch, result = refs[:-2], refs[-2], refs[-1]
    c, xl, y = pos[0], pos[1], pos[3]
    for ref, side in ((own_ref, xl), (far_ref, 1 - xl)):
        scratch[2 * side + c] = ref[0]
        scratch[2 * side + 1 - c] = ref[1]
    groups, per, _ = scratch.shape
    a = scratch[...].reshape(groups * per, scratch.shape[2])
    width = LANES
    quarters = w_ref.shape[1] // width

    def weights(i):
        rows = w_ref[i * width : (i + 1) * width, :]
        return jnp.concatenate([rows[:, q * width : (q + 1) * width] for q in range(quarters)], 0)

    for i in range(0, w_ref.shape[0] // width, 2):
        w = jnp.concatenate([weights(i), weights(i + 1)], 1)
        got = jnp.dot(a, w, preferred_element_type=F32).astype(BF16)
        result[:, :, i * width : (i + 2) * width] = got.reshape(groups, per, 2 * width)
    for k, ref in enumerate(outs):
        ref[...] = result[lax.bitwise_xor(y, k)]


def qkv_body(loc_dev, head_dim, pos, own_ref, y1_ref, y2_ref, y3_ref, gain_ref, w_ref, keep_ref, send_ref, scratch):
    c, y = pos[0], pos[3]
    for k, ref in enumerate((own_ref, y1_ref, y2_ref, y3_ref)):
        scratch[lax.bitwise_xor(y, k)] = ref[...]
    groups, per, model = scratch.shape
    rows = groups * per
    columns = w_ref.shape[1] // 3
    start = pl.multiple_of(c * LANES, LANES)
    gain = gain_ref[0, :, pl.ds(start, LANES)]
    gain = jnp.concatenate([gain[i : i + 1] for i in range(gain.shape[0])], 1)
    hi = rounded(gain)
    mid = rounded(gain - hi)
    row = lax.broadcasted_iota(jnp.int32, (16, model), 0)
    extra = jnp.where(row == 0, hi, jnp.where(row == 1, mid, jnp.where(row == 2, gain - hi - mid, 0.0)))
    a_f = scratch[...].reshape(rows, model).astype(F32)
    mean = jnp.mean(a_f, axis=1, keepdims=True)
    dev = a_f - mean
    spread = jnp.sum(dev * dev, axis=1, keepdims=True)
    lhs = jnp.concatenate([(dev * gain).astype(BF16), extra.astype(BF16)], 0)
    got = jnp.dot(lhs, w_ref[...], preferred_element_type=F32)
    column_sums = got[rows : rows + 1] + got[rows + 1 : rows + 2] + got[rows + 2 : rows + 3]
    got = got[:rows] + mean * column_sums
    at = lane((rows, LANES))
    wide = jnp.where(at == 0, mean, jnp.where(at == 1, spread, jnp.where(at == 2, mean * mean, 0.0)))
    stats = jnp.transpose(wide)
    base = 2 * rows + 4 * Q_DEV

    def write(ref, x, h):
        for i in (0, 1):
            ref[x, i * rows : (i + 1) * rows, :] = got[:rows, i * columns + h * head_dim : i * columns + (h + 1) * head_dim]
        lo = 2 * columns + h * head_dim
        for w in range(4):
            ref[x, 2 * rows + w * Q_DEV : 2 * rows + (w + 1) * Q_DEV, :] = got[w * loc_dev : w * loc_dev + Q_DEV, lo : lo + head_dim]
        for i in range(3):
            lo = i * columns + h * head_dim
            ref[x, base + i : base + i + 1, :] = column_sums[:, lo : lo + head_dim]
        ref[x, base + 3 : base + 8, :] = stats[:5]

    for x in (0, 1):
        for core in (0, 1):
            @pl.when(c == core)
            def _():
                write(keep_ref, x, 2 * x + core)

            @pl.when(c != core)
            def _():
                write(send_ref, x, 2 * x + core)


def shift(x, axis, by):
    n = lax.axis_size(axis)
    return lax.ppermute(x, axis, [(i, (i + by) % n) for i in range(n)])


def flip(x, axis, bits):
    return lax.ppermute(x, axis, [(i, i ^ bits) for i in range(lax.axis_size(axis))])


def by_bit(bit, mine, other):
    return jnp.where(bit == 0, jnp.stack([mine, other]), jnp.stack([other, mine]))


def pick(x, i):
    return lax.dynamic_index_in_dim(x, i, 0, keepdims=False)


def on_device(tokens, slab_index, agg_query, agg_key_w, agg_value_w, agg_out_w, norm_gain, query_w, key_w, value_w):
    model = tokens.shape[2]
    rows_w, columns = agg_key_w.shape
    head_dim = model // HEADS
    heads = columns // head_dim
    factor = 1.0 / math.sqrt(head_dim)
    n_z = lax.axis_size("z")
    locs = tokens.shape[1]
    loc_dev = locs // (4 * n_z)
    xl, z, c = lax.axis_index("xl"), lax.axis_index("z"), lax.axis_index("c")
    y, xh = lax.axis_index("y"), lax.axis_index("xh")
    wide = lax.axis_index(WIDE)
    toks = tokens.reshape(locs, model)
    zs = [lax.rem(z + k, n_z) for k in range(n_z)]
    pos = jnp.stack([c, xl, z, y, xh, wide, slab_index[0], *zs]).astype(jnp.int32)

    out_blocks = [agg_out_w[i : i + rows_w] for i in range(0, columns, rows_w)]
    later = side_by_side([key_w, value_w, query_w, *out_blocks])

    own_head = jnp.arange(columns)[None, :] // head_dim == jnp.arange(heads)[:, None]
    q_diag = jnp.where(own_head, agg_query[None, :], 0).astype(BF16)
    merged = factor * lax.dot_general(q_diag, agg_key_w, NT, preferred_element_type=F32)
    parts = jnp.concatenate([*split3(merged), jnp.zeros((PARTS - 3 * heads, rows_w), BF16)], 0)
    packed = jnp.concatenate([agg_value_w, jnp.pad(parts, ((0, 0), (0, columns - rows_w)))], 0)

    def stack(blocks, axis, after):
        if axis:
            shape = blocks[0].shape[:1] + (columns,)
            return call(side_body, pos, sds((1,) + shape, BF16), [full(b.shape) for b in blocks], full((1,) + shape), blocks, after=after)
        shape = (len(blocks),) + blocks[0].shape
        return call(stack_body, pos, sds(shape, BF16), [full(b.shape) for b in blocks], full(shape), blocks, after=after)

    at = {}

    def join(lot, after=()):
        shape = (sum(b.shape[0] for b in lot),) + packed.shape
        return call(join_body, pos, sds(shape, BF16), [full(b.shape) for b in lot], full(shape), lot, after=after)

    def over_cores(lot, joined):
        swapped = shift(joined, "c", 1)
        start = 0
        for block in lot:
            at[id(block)] = (swapped, start)
            start += block.shape[0]
        return swapped

    ups, downs, owns, fars = [packed], [packed], [packed[None]], [shift(packed[None], "xl", 1)]
    lots, joins = [], []
    for k in range(1, n_z // 2):
        ups.append(shift(ups[-1], "z", 1))
        downs.append(shift(downs[-1], "z", -1))
        if k == 3:
            lots.append([owns[0], fars[0], owns[1], fars[1]])
            joins.append(join(lots[0]))
        owns.append(stack((ups[-1], downs[-1]), 0, [*fars[-1:], *([later] if k == 1 else joins)]))
        fars.append(shift(owns[-1], "xl", 1))
    first = shift(ups[-1][:, : columns // 2], "z", 1)
    second = shift(downs[-1][:, columns // 2 :], "z", -1)
    lots.append([owns[2], fars[2], owns[3]])
    joins.append(join(lots[1]))
    over_cores(lots[0], joins[0])
    owns.append(stack((first, second), 1, [fars[-1], joins[1], at[id(owns[0])][0]]))
    over_cores(lots[1], joins[1])
    fars.append(shift(owns[-1], "xl", 1))
    weights_z = lax.all_gather(once(later, owns[2]), "z", axis=0, tiled=True)

    def chunk(offset, k, i):
        rows = []
        for block in (owns[k], fars[k]):
            other, start = at[id(block)]
            rows.append([(block, i), (other, start + i)])
        return offset, rows

    chunks = [chunk(0, 0, 0)]
    for k in (1, 2):
        chunks += [chunk(n_z - k, k, 0), chunk(k, k, 1)]
    acc = value_call(pos, toks, chunks, None, False, heads, loc_dev, False)
    lot = [fars[3], owns[4], fars[4]]
    over_cores(lot, join(lot, after=acc[1:]))
    chunks += [chunk(n_z - 3, 3, 0), chunk(3, 3, 1), chunk(4, 4, 0)]

    half = locs // 4
    ext = columns + LANES
    flat = lambda x: x.reshape(half, x.shape[-1])
    msg, v, s = value_call(pos, toks, chunks[5:], acc, True, heads, loc_dev, False)
    args = (flat(v), flat(s), flat(shift(msg, "c", 1)))
    shape = (half + half // 16, columns)
    gone = call(functools.partial(first_body, heads), pos, sds(shape, BF16), [full(a.shape) for a in args], full(shape), args)
    far_msg = shift(gone, "xl", 1)
    msg, v, s = value_call(pos, toks, chunks, None, True, heads, loc_dev, True, after=(gone,))
    two = [x.reshape(half // 2, ext) for x in (shift(msg[: n_z // 2], "c", 1), shift(msg[n_z // 2 :], "c", 1))]
    args = (flat(v), flat(s), far_msg, *two)
    msg = call(functools.partial(last_body, heads), pos, sds((half, ext), BF16), [full(a.shape) for a in args], full((half, ext)), args)
    msg = lax.all_to_all(msg.reshape(n_z, loc_dev, ext), "z", 0, 0, tiled=True)
    agg = call(
        functools.partial(ring_body, heads),
        pos,
        sds((loc_dev, columns), BF16),
        [full(msg.shape)],
        full((loc_dev, columns)),
        (msg,),
        scratch=[pltpu.VMEM((2 * loc_dev, columns), F32)],
    )

    near = jnp.stack([agg, shift(agg, "c", 1)])
    far = shift(near, "xl", 1)
    n_rows = 4 * loc_dev
    part = n_z * rows_w
    block = (loc_dev, part)
    sent = call(
        out_body,
        pos,
        [sds(block, BF16)] * 4,
        [full(near.shape), full(far.shape), full((part, columns))],
        [full(block)] * 4,
        (near, far, weights_z[:, 3 * columns :]),
        scratch=[pltpu.VMEM((4, loc_dev, columns), BF16), pltpu.VMEM((4,) + block, BF16)],
    )
    got = [flip(sent[k], "y", k) for k in (1, 2, 3)]
    mine = sum(x.astype(F32) for x in (sent[0], *got))
    mine = (mine + shift(mine.astype(BF16), "xh", 1).astype(F32)).astype(BF16)
    others = [flip(mine, "y", k) for k in (1, 2, 3)]

    base = 2 * n_rows + 4 * Q_DEV
    sums_shape = (2, base + 8, head_dim)
    keep, send = call(
        functools.partial(qkv_body, loc_dev, head_dim),
        pos,
        [sds(sums_shape, F32)] * 2,
        [full(mine.shape)] * 4
        + [pl.BlockSpec((1, n_z, 2 * rows_w), lambda i, s: (s[1], 0, 0))]
        + [full((part, 3 * columns))],
        [full(sums_shape)] * 2,
        (mine, *others, norm_gain.reshape(2, n_z, 2 * rows_w), weights_z[:, : 3 * columns]),
        scratch=[pltpu.VMEM((4,) + block, BF16)],
    )
    sums = keep + shift(send, "c", 1)
    sums = pick(sums, xl) + shift(pick(sums, 1 - xl), "xl", 1)
    col = sums[base : base + 3]
    mean_all = sums[base + 3] / 4
    between = sums[base + 5] / 4 - mean_all * mean_all
    var = sums[base + 4] / model + jnp.maximum(between, 0.0)
    rstd = lax.rsqrt(var + 1e-05)

    def normed(x, i, m, r):
        return ((x - m[:, None] * col[i][None, :]) * r[:, None]).astype(BF16)

    slab_of = lambda x: x.reshape(4, loc_dev)[:, :Q_DEV].reshape(-1)
    key_out = normed(sums[:n_rows], 0, mean_all, rstd)
    value_out = normed(sums[n_rows : 2 * n_rows], 1, mean_all, rstd)
    query_out = normed(sums[2 * n_rows : base], 2, slab_of(mean_all), slab_of(rstd))

    kv = jnp.concatenate([key_out, value_out], 1)
    kv_all = jnp.concatenate([kv, flip(kv, "z", 2), flip(kv, "z", 4), flip(kv, "z", 6)], 0)
    both = jnp.concatenate([query_out, flip(query_out, "z", 1)], 0)
    scores = factor * lax.dot_general(both, kv_all[:, :head_dim], NT, preferred_element_type=F32)
    top = jnp.max(scores, axis=-1, keepdims=True)
    powers = jnp.exp(scores - top)
    total = jnp.sum(powers, axis=-1, keepdims=True)
    part_out = jnp.dot(powers, kv_all[:, head_dim:].astype(F32), precision=lax.Precision.HIGHEST)
    half_lanes = (part_out.shape[0], head_dim // 2)
    ends = jnp.concatenate([part_out, jnp.broadcast_to(top, half_lanes), jnp.broadcast_to(total, half_lanes)], 1)
    ends = jnp.moveaxis(ends.reshape(2, 2, 2, Q_DEV, 2 * head_dim), 2, 0)
    ends = by_bit(c, pick(ends, c), shift(pick(ends, 1 - c), "c", 1))
    ends = jnp.moveaxis(ends, 2, 0)
    near, far = pick(ends, xl), pick(ends, 1 - xl)
    cross = [(x * n_z + i, (1 - x) * n_z + (i ^ 1)) for x in (0, 1) for i in range(n_z)]
    here = by_bit(xl, near[:, 0], shift(far[:, 0], "xl", 1))
    there = by_bit(xl, flip(near[:, 1], "z", 1), lax.ppermute(far[:, 1], ("xl", "z"), cross))
    tops = [e[..., head_dim : head_dim + 1] for e in (here, there)]
    best = jnp.maximum(*tops)
    scales = [jnp.exp(t - best) for t in tops]
    total = sum(f * e[..., -1:] for f, e in zip(scales, (here, there)))
    attended = sum(f * e[..., :head_dim] for f, e in zip(scales, (here, there))) / total
    return jnp.moveaxis(attended.reshape(heads, Q_DEV, head_dim), 1, 0).reshape(Q_DEV, columns).astype(BF16)


def solution(mesh):
    n_z = mesh.devices.shape[0] // 4
    fine = Mesh(mesh.devices.reshape(2, n_z, 2, 4, 2), WIDE + HEAD)
    placed = (
        P(WIDE, None, None),
        P(WIDE),
        P(HEAD),
        P(WIDE, HEAD),
        P(WIDE, HEAD),
        P(HEAD, WIDE),
        P(),
        P(WIDE, HEAD),
        P(WIDE, HEAD),
        P(WIDE, HEAD),
    )
    return jax.shard_map(on_device, mesh=fine, in_specs=placed, out_specs=P(WIDE, HEAD), check_vma=False)
```

time: 198 us -> 164 us (0.83)
  waiting for transfers between devices: 53.4 us -> 32.9 us
  blocking collectives: 30.8 us -> 17.5 us
  Pallas kernels: 28.6 us -> 23.8 us
  local copies, waits for them, and re-layouts: 4.53 us -> 6.57 us
    ppermute x37 -> x27, waiting for transfers between devices: 52.7 us -> 22.5 us  [shift(): return lax.ppermute(x, axis, [(i, (i + by) % n) for i in range(n)])]
    ppermute x0 -> x12, starting transfers between devices: none -> 18.5 us  [the longest x11 18.4 us: flip(): lax.ppermute(x, axis, [(i, i ^ bits) for i in range(lax.axis_size(axis))])]
    ppermute x37 -> x27, starting transfers between devices: 61.4 us -> 44.6 us  [shift(): return lax.ppermute(x, axis, [(i, (i + by) % n) for i in range(n)])]
    all_to_all x1 -> x0, blocking collectives: 14.6 us -> none  [on_device(): got = lax.all_to_all(partial_sum, HEAD, 0, 0, tiled=True)]
    ppermute x0 -> x12, waiting for transfers between devices: none -> 10.3 us  [the longest x11 7.98 us: flip(): lax.ppermute(x, axis, [(i, i ^ bits) for i in range(lax.axis_size(axis))])]
    pallas_call x11 -> x16, Pallas kernels: 28.6 us -> 23.8 us  [the longest x15 23.8 us: call(): pl.pallas_call(kernel, out_shape=out_shape, grid_spec=pltpu.PrefetchScala...]
    slice x0 -> x6, local copies, waits for them, and re-layouts: none -> 4.25 us  [the longest x1 2.09 us: on_device(): weights_z[:, :3 * columns]]
  transfers between devices with their start and end apart: 39 -> 40, of which waited for: 21 -> 21; matrix products, arithmetic and copies ran while one was open for 2% -> 4% of each run, Pallas kernels for 14% -> 12%
where the time goes in v2:
time: 164 us
  starting transfers between devices  63.1 us (38%)
  waiting for transfers between devices  32.9 us (20%)
  Pallas kernels  23.8 us (15%)
  blocking collectives  17.5 us (11%)
  between operations  14.5 us (9%)
  local copies, waits for them, and re-layouts  6.57 us (4%)
  other arithmetic  3.88 us (2%)
    ppermute x27, starting transfers between devices, shift(): return lax.ppermute(x, axis, [(i, (i + by) % n) for i in range(n)])  44.6 us
    pallas_call x15, Pallas kernels, call(): pl.pallas_call(kernel, out_shape=out_shape, grid_spec=pltpu.PrefetchScala...  23.8 us
    ppermute x27, waiting for transfers between devices, shift(): return lax.ppermute(x, axis, [(i, (i + by) % n) for i in range(n)])  22.5 us
    ppermute x11, starting transfers between devices, flip(): lax.ppermute(x, axis, [(i, i ^ bits) for i in range(lax.axis_size(axis))])  18.4 us
    all_to_all x1, blocking collectives, on_device(): msg = lax.all_to_all(msg.reshape(n_z, loc_dev, ext), 'z', 0, 0, tiled=True)  17.5 us
    ppermute x11, waiting for transfers between devices, flip(): lax.ppermute(x, axis, [(i, i ^ bits) for i in range(lax.axis_size(axis))])  7.98 us
  transfers between devices with their start and end apart: 40, of which 21 were waited for; matrix products, arithmetic and copies ran while one was open for 4% of the time, Pallas kernels for 12%

profile of v2, /device:TPU:1, one launch (start us, length us, event | category | flops | bytes accessed | tf_op | source)
XLA Modules:
  0.0 163.6 jit_solution(3514937132616967698)
XLA Ops:
  6.6 0.8 copy-done
  7.4 0.8 reduce-precision_convert_fusion.1
  8.3 0.9 fusion.1
  9.3 2.5 %collective-permute-start.1 = (bf16[144,512]{1,0:T(8,128)(2,1)S(1)}, bf16[144,512]{1,0:T(8,128)(2,1)S(1)}, u32[]{:S(2)}, u32[]{:S(2)}) collective-permute-start(bf16[144,512]{1,0:T(8,128)(2,1)S(1)} %get-tuple-element.50), channel_id=1, source_target_pairs={{0,16},{16,32},{32,48},{48,64},{64,80},{80,96},{96,112},{112,0},{1... | collective-permute-start | bytes 442376 | tf_op jit(solution)/shard_map/ppermute | solution.py:345
  11.8 4.0 %collective-permute-start.2 = (bf16[144,512]{1,0:T(8,128)(2,1)S(1)}, bf16[144,512]{1,0:T(8,128)(2,1)S(1)}, u32[]{:S(2)}, u32[]{:S(2)}) collective-permute-start(bf16[144,512]{1,0:T(8,128)(2,1)S(1)} %get-tuple-element.50), channel_id=1, source_target_pairs={{0,112},{16,0},{32,16},{48,32},{64,48},{80,64},{96,80},{112,96},{1... | collective-permute-start | bytes 442376 | tf_op jit(solution)/shard_map/ppermute | solution.py:345
  15.8 1.2 collective-permute-start
  17.1 0.8 fusion.46
  17.9 1.3 select_select_fusion.refs_3_.refs_0_
  20.8 1.3 collective-permute-start.3
  22.1 2.7 %collective-permute-start.6 = (bf16[144,512]{1,0:T(8,128)(2,1)S(1)}, bf16[144,512]{1,0:T(8,128)(2,1)S(1)}, u32[]{:S(2)}, u32[]{:S(2)}) collective-permute-start(bf16[144,512]{1,0:T(8,128)(2,1)S(1)} %collective-permute-done.2.refs_1_), channel_id=1, source_target_pairs={{0,112},{16,0},{32,16},{48,32},{64,48},{80,64},{96,80},{112,96},{1... | collective-permute-start | bytes 442376 | tf_op jit(solution)/shard_map/ppermute | solution.py:345
  24.8 2.5 %collective-permute-done.5.refs_0_ = bf16[144,512]{1,0:T(8,128)(2,1)S(1)} collective-permute-done((bf16[144,512]{1,0:T(8,128)(2,1)S(1)}, bf16[144,512]{1,0:T(8,128)(2,1)S(1)}, u32[]{:S(2)}, u32[]{:S(2)}) %collective-permute-start.5) | collective-permute-done | bytes 147488 | tf_op jit(solution)/shard_map/ppermute | solution.py:345
  28.1 0.7 copy-done.2
  28.9 1.3 collective-permute-start.7
  30.2 2.7 %collective-permute-start.9 = (bf16[144,512]{1,0:T(8,128)(2,1)S(1)}, bf16[144,512]{1,0:T(8,128)(2,1)S(1)}, u32[]{:S(2)}, u32[]{:S(2)}) collective-permute-start(bf16[144,512]{1,0:T(8,128)(2,1)S(1)} %collective-permute-done.6.refs_1_), channel_id=1, source_target_pairs={{0,112},{16,0},{32,16},{48,32},{64,48},{80,64},{96,80},{112,96},{1... | collective-permute-start | bytes 442376 | tf_op jit(solution)/shard_map/ppermute | solution.py:345
  33.5 3.7 %collective-permute-start.4 = (bf16[6,144,512]{2,1,0:T(8,128)(2,1)S(1)}, bf16[6,144,512]{2,1,0:T(8,128)(2,1)S(1)}, u32[]{:S(2)}, u32[]{:S(2)}) collective-permute-start(bf16[6,144,512]{2,1,0:T(8,128)(2,1)S(1)} %shard_map.101.refs_3_), channel_id=1, source_target_pairs={{0,8},{8,0},{1,9},{9,1},{2,10},{10,2},{3,11},{11,3},{4,12},{12,4},... | collective-permute-start | bytes 2654216 | tf_op jit(solution)/shard_map/ppermute | solution.py:345
  38.4 2.5 %collective-permute-start.10 = (bf16[6,144,512]{2,1,0:T(8,128)(2,1)S(1)}, bf16[6,144,512]{2,1,0:T(8,128)(2,1)S(1)}, u32[]{:S(2)}, u32[]{:S(2)}) collective-permute-start(bf16[6,144,512]{2,1,0:T(8,128)(2,1)S(1)} %shard_map.104.refs_3_), channel_id=1, source_target_pairs={{0,8},{8,0},{1,9},{9,1},{2,10},{10,2},{3,11},{11,3},{4,12},{12,4},... | collective-permute-start | bytes 2654216 | tf_op jit(solution)/shard_map/ppermute | solution.py:345
  41.4 2.5 %collective-permute-start.12 = (bf16[144,256]{1,0:T(8,128)(2,1)S(1)}, bf16[144,256]{1,0:T(8,128)(2,1)S(1)}, u32[]{:S(2)}, u32[]{:S(2)}) collective-permute-start(bf16[144,256]{1,0:T(8,128)(2,1)S(1)} %slice.136), channel_id=1, source_target_pairs={{0,16},{16,32},{32,48},{48,64},{64,80},{80,96},{96,112},{112,0},{1... | collective-permute-start | bytes 221192 | tf_op jit(solution)/shard_map/ppermute | solution.py:345
  44.5 2.5 %collective-permute-done.12.refs_0_ = bf16[144,256]{1,0:T(8,128)(2,1)S(1)} collective-permute-done((bf16[144,256]{1,0:T(8,128)(2,1)S(1)}, bf16[144,256]{1,0:T(8,128)(2,1)S(1)}, u32[]{:S(2)}, u32[]{:S(2)}) %collective-permute-start.12) | collective-permute-done | bytes 73760 | tf_op jit(solution)/shard_map/ppermute | solution.py:345
  47.0 2.8 %collective-permute-done.13.refs_1_ = bf16[144,256]{1,0:T(8,128)(2,1)S(1)} collective-permute-done((bf16[144,256]{1,0:T(8,128)(2,1)S(1)}, bf16[144,256]{1,0:T(8,128)(2,1)S(1)}, u32[]{:S(2)}, u32[]{:S(2)}) %collective-permute-start.13) | collective-permute-done | bytes 73760 | tf_op jit(solution)/shard_map/ppermute | solution.py:345
  50.9 4.5 %shard_map.106 = (f32[512,512]{1,0:T(8,128)S(1)}, f32[512,128]{1,0:T(8,128)S(1)}) custom-call(s32[15]{0:T(128)S(1)} %stack.104.pos, bf16[1024,4096]{1,0:T(8,128)(2,1)} %bitcast.101, bf16[1024,4096]{1,0:T(8,128)(2,1)} %bitcast.102, bf16[1024,4096]{1,0:T(8,128)(2,1)} %bitcast.103, bf16[1024,4096]{1,0:T(8,128)(2,1)} %bitcast.104, bf16[1024,4096]{1,0:T(8,128)(2,1)} %bitcast.105, ...), custom_call_target="tpu_custom_call" | custom-call | flops 1 | bytes 1 | tf_op jit(solution)/shard_map/pallas_call | solution.py:29
  56.0 1.6 collective-permute-start.15
  57.6 1.6 collective-permute-done.15.refs_9_.refs_26_
  59.2 3.3 %shard_map.108 = (bf16[8,32,640]{2,1,0:T(8,128)(2,1)S(1)}, f32[8,32,512]{2,1,0:T(8,128)S(1)}, f32[8,32,128]{2,1,0:T(8,128)S(1)}) custom-call(s32[15]{0:T(128)S(1)} %stack.104.pos, bf16[1024,4096]{1,0:T(8,128)(2,1)} %bitcast.116, bf16[1024,4096]{1,0:T(8,128)(2,1)} %bitcast.112, bf16[1024,4096]{1,0:T(8,128)(2,1)} %bitcast.113, bf16[1024,4096]{1,0:T(8,128)(2,1)} %bitcast.114, ...), custom_call_target="tpu_custom_call" | custom-call | flops 1 | bytes 1 | tf_op jit(solution)/shard_map/pallas_call | solution.py:29
  63.0 1.3 collective-permute-done.16
  64.2 1.1 shard_map.109.refs_29_
  65.4 1.2 collective-permute-start.17
  66.6 6.4 %shard_map.110 = (bf16[8,32,640]{2,1,0:T(8,128)(2,1)S(1)}, f32[8,32,512]{2,1,0:T(8,128)S(1)}, f32[8,32,128]{2,1,0:T(8,128)S(1)}) custom-call(s32[15]{0:T(128)S(1)} %stack.104.pos, bf16[1024,4096]{1,0:T(8,128)(2,1)} %bitcast.117, bf16[1024,4096]{1,0:T(8,128)(2,1)} %bitcast.118, bf16[1024,4096]{1,0:T(8,128)(2,1)} %bitcast.119, bf16[1024,4096]{1,0:T(8,128)(2,1)} %bitcast.120, ...), custom_call_target="tpu_custom_call" | custom-call | flops 1 | bytes 1 | tf_op jit(solution)/shard_map/pallas_call | solution.py:29
  73.0 0.7 collective-permute-start.18
  73.8 0.9 collective-permute-done.18
  75.1 1.3 shard_map.111
  76.4 17.5 %all_to_all.5.msg_ref = bf16[8,32,640]{2,1,0:T(8,128)(2,1)S(1)} all-to-all(bf16[8,32,640]{2,1,0:T(8,128)(2,1)S(1)} %bitcast.92), channel_id=1, replica_groups=mesh['xl'=2,'z'=8,'c'=2,'y'=4,'xh'=2] {'z'}, dimensions={0} | all-to-all | bytes 655360 | tf_op jit(solution)/shard_map/all_to_all | solution.py:453
  93.9 0.9 shard_map.112
  94.9 1.1 collective-permute-start.20
  96.0 0.9 collective-permute-done.20
  96.9 1.1 collective-permute-start.21
  97.9 1.3 slice.138.w_ref
  99.2 0.8 collective-permute-done.21.far_ref
  100.0 0.9 shard_map.114
  100.9 1.4 collective-permute-start.22
  102.3 2.6 %collective-permute-start.23 = (bf16[32,1024]{1,0:T(8,128)(2,1)S(1)}, bf16[32,1024]{1,0:T(8,128)(2,1)S(1)}, u32[]{:S(2)}, u32[]{:S(2)}) collective-permute-start(bf16[32,1024]{1,0:T(8,128)(2,1)S(1)} %get-tuple-element.29), channel_id=1, source_target_pairs={{0,4},{2,6},{4,0},{6,2},{1,5},{3,7},{5,1},{7,3},{8,12},{10,14},{12... | collective-permute-start | bytes 196616 | tf_op jit(solution)/shard_map/ppermute | solution.py:349
  104.9 2.3 %collective-permute-done.23 = bf16[32,1024]{1,0:T(8,128)(2,1)S(1)} collective-permute-done((bf16[32,1024]{1,0:T(8,128)(2,1)S(1)}, bf16[32,1024]{1,0:T(8,128)(2,1)S(1)}, u32[]{:S(2)}, u32[]{:S(2)}) %collective-permute-start.23) | collective-permute-done | bytes 65568 | tf_op jit(solution)/shard_map/ppermute | solution.py:349
  107.2 2.7 %collective-permute-done.24 = bf16[32,1024]{1,0:T(8,128)(2,1)S(1)} collective-permute-done((bf16[32,1024]{1,0:T(8,128)(2,1)S(1)}, bf16[32,1024]{1,0:T(8,128)(2,1)S(1)}, u32[]{:S(2)}, u32[]{:S(2)}) %collective-permute-start.24) | collective-permute-done | bytes 65568 | tf_op jit(solution)/shard_map/ppermute | solution.py:349
  110.0 2.6 %collective-permute-start.25 = (bf16[32,1024]{1,0:T(8,128)(2,1)S(1)}, bf16[32,1024]{1,0:T(8,128)(2,1)S(1)}, u32[]{:S(2)}, u32[]{:S(2)}) collective-permute-start(bf16[32,1024]{1,0:T(8,128)(2,1)S(1)} %fusion.11), channel_id=1, source_target_pairs={{0,1},{1,0},{2,3},{3,2},{4,5},{5,4},{6,7},{7,6},{8,9},{9,8},{10,11... | collective-permute-start | bytes 196616 | tf_op jit(solution)/shard_map/ppermute | solution.py:345
  112.5 2.1 %collective-permute-done.25 = bf16[32,1024]{1,0:T(8,128)(2,1)S(1)} collective-permute-done((bf16[32,1024]{1,0:T(8,128)(2,1)S(1)}, bf16[32,1024]{1,0:T(8,128)(2,1)S(1)}, u32[]{:S(2)}, u32[]{:S(2)}) %collective-permute-start.25) | collective-permute-done | bytes 65568 | tf_op jit(solution)/shard_map/ppermute | solution.py:345
  114.8 1.0 collective-permute-start.27
  115.8 2.9 %collective-permute-start.28 = (bf16[32,1024]{1,0:T(8,128)(2,1)S(1)}, bf16[32,1024]{1,0:T(8,128)(2,1)S(1)}, u32[]{:S(2)}, u32[]{:S(2)}) collective-permute-start(bf16[32,1024]{1,0:T(8,128)(2,1)S(1)} %add_convert_fusion.own_ref), channel_id=1, source_target_pairs={{0,6},{2,4},{4,2},{6,0},{1,7},{3,5},{5,3},{7,1},{8,14},{10,12},{12... | collective-permute-start | bytes 196616 | tf_op jit(solution)/shard_map/ppermute | solution.py:349
  118.7 2.1 %slice.139.w_ref = bf16[1024,1536]{1,0:T(8,128)(2,1)S(1)} slice(bf16[1024,2048]{1,0:T(8,128)(2,1)} %all-gather.2.cloned.1.call-done), slice={[0:1024], [0:1536]} | slice | bytes 6291456 | tf_op jit(solution)/shard_map/slice | solution.py:493
  120.8 1.4 shard_map.115
  122.2 5.0 %collective-permute-start.29 = (f32[2,296,128]{2,1,0:T(8,128)S(1)}, f32[2,296,128]{2,1,0:T(8,128)S(1)}, u32[]{:S(2)}, u32[]{:S(2)}) collective-permute-start(f32[2,296,128]{2,1,0:T(8,128)S(1)} %get-tuple-element.32), channel_id=1, source_target_pairs={{0,8},{8,0},{1,9},{9,1},{2,10},{10,2},{3,11},{11,3},{4,12},{12,4},... | collective-permute-start | bytes 909320 | tf_op jit(solution)/shard_map/ppermute | solution.py:345
  127.2 1.2 collective-permute-done.29
  128.5 1.1 collective-permute-start.30
  129.6 4.2 %collective-permute-done.30 = f32[296,128]{1,0:T(8,128)S(1)} collective-permute-done((f32[296,128]{1,0:T(8,128)S(1)}, f32[296,128]{1,0:T(8,128)S(1)}, u32[]{:S(2)}, u32[]{:S(2)}) %collective-permute-start.30) | collective-permute-done | bytes 151584 | tf_op jit(solution)/shard_map/ppermute | solution.py:345
  134.0 2.9 %collective-permute-start.32 = (bf16[128,256]{1,0:T(8,128)(2,1)S(1)}, bf16[128,256]{1,0:T(8,128)(2,1)S(1)}, u32[]{:S(2)}, u32[]{:S(2)}) collective-permute-start(bf16[128,256]{1,0:T(8,128)(2,1)S(1)} %pad_maximum_fusion.2), channel_id=1, source_target_pairs={{0,32},{16,48},{32,0},{48,16},{64,96},{80,112},{96,64},{112,80},{1... | collective-permute-start | bytes 196616 | tf_op jit(solution)/shard_map/ppermute | solution.py:349
  136.8 2.1 %collective-permute-start.33 = (bf16[128,256]{1,0:T(8,128)(2,1)S(1)}, bf16[128,256]{1,0:T(8,128)(2,1)S(1)}, u32[]{:S(2)}, u32[]{:S(2)}) collective-permute-start(bf16[128,256]{1,0:T(8,128)(2,1)S(1)} %pad_maximum_fusion.2), channel_id=1, source_target_pairs={{0,64},{16,80},{32,96},{48,112},{64,0},{80,16},{96,32},{112,48},{1... | collective-permute-start | bytes 196616 | tf_op jit(solution)/shard_map/ppermute | solution.py:349
  138.9 1.3 collective-permute-start.34
  140.7 2.4 %collective-permute-start.31 = (bf16[32,128]{1,0:T(8,128)(2,1)S(1)}, bf16[32,128]{1,0:T(8,128)(2,1)S(1)}, u32[]{:S(2)}, u32[]{:S(2)}) collective-permute-start(bf16[32,128]{1,0:T(8,128)(2,1)S(1)} %fusion.19), channel_id=1, source_target_pairs={{0,16},{16,0},{32,48},{48,32},{64,80},{80,64},{96,112},{112,96},{1... | collective-permute-start | bytes 24584 | tf_op jit(solution)/shard_map/ppermute | solution.py:349
  143.1 1.6 collective-permute-done.33
  146.1 2.5 %collective-permute-start.35 = (f32[2,2,8,256]{3,2,1,0:T(8,128)S(1)}, f32[2,2,8,256]{3,2,1,0:T(8,128)S(1)}, u32[]{:S(2)}, u32[]{:S(2)}) collective-permute-start(f32[2,2,8,256]{3,2,1,0:T(8,128)S(1)} %get-tuple-element.59), channel_id=1, source_target_pairs={{0,8},{8,0},{1,9},{9,1},{2,10},{10,2},{3,11},{11,3},{4,12},{12,4},... | collective-permute-start | bytes 98312 | tf_op jit(solution)/shard_map/ppermute | solution.py:345
  148.6 0.9 collective-permute-done.35
  149.4 1.1 collective-permute-start.36
  150.5 1.8 %collective-permute-start.37 = (f32[2,8,256]{2,1,0:T(8,128)S(1)}, f32[2,8,256]{2,1,0:T(8,128)S(1)}, u32[]{:S(2)}, u32[]{:S(2)}) collective-permute-start(f32[2,8,256]{2,1,0:T(8,128)S(1)} %get-tuple-element.61), channel_id=1, source_target_pairs={{0,16},{16,0},{32,48},{48,32},{64,80},{80,64},{96,112},{112,96},{1... | collective-permute-start | bytes 49160 | tf_op jit(solution)/shard_map/ppermute | solution.py:349
  152.5 1.0 collective-permute-done.37
  153.5 2.4 %collective-permute-done.38 = f32[2,8,256]{2,1,0:T(8,128)S(1)} collective-permute-done((f32[2,8,256]{2,1,0:T(8,128)S(1)}, f32[2,8,256]{2,1,0:T(8,128)S(1)}, u32[]{:S(2)}, u32[]{:S(2)}) %collective-permute-start.38) | collective-permute-done | bytes 16416 | tf_op jit(solution)/shard_map/ppermute | solution.py:528
  156.0 0.7 fusion.23
  (95 shorter events, 10.1 us)
Async XLA Ops:
  6.5 0.9 copy-start
  6.5 91.4 %all-gather.2.cloned.1.call-start = ((), (), s32[]{:S(2)}) async-start(), calls=%async_computation.1 | async-start | bytes 4718592 | tf_op jit(solution)/shard_map/all_gather | solution.py:424
  9.3 11.0 %collective-permute-start.1 = (bf16[144,512]{1,0:T(8,128)(2,1)S(1)}, bf16[144,512]{1,0:T(8,128)(2,1)S(1)}, u32[]{:S(2)}, u32[]{:S(2)}) collective-permute-start(bf16[144,512]{1,0:T(8,128)(2,1)S(1)} %get-tuple-element.50), channel_id=1, source_target_pairs={{0,16},{16,32},{32,48},{48,64},{64,80},{80,96},{96,112},{112,0},{1... | collective-permute-start | bytes 442376 | tf_op jit(solution)/shard_map/ppermute | solution.py:345
  11.8 8.4 %collective-permute-start.2 = (bf16[144,512]{1,0:T(8,128)(2,1)S(1)}, bf16[144,512]{1,0:T(8,128)(2,1)S(1)}, u32[]{:S(2)}, u32[]{:S(2)}) collective-permute-start(bf16[144,512]{1,0:T(8,128)(2,1)S(1)} %get-tuple-element.50), channel_id=1, source_target_pairs={{0,112},{16,0},{32,16},{48,32},{64,48},{80,64},{96,80},{112,96},{1... | collective-permute-start | bytes 442376 | tf_op jit(solution)/shard_map/ppermute | solution.py:345
  15.8 4.4 %collective-permute-start = (bf16[1,144,512]{2,1,0:T(8,128)(2,1)S(1)}, bf16[1,144,512]{2,1,0:T(8,128)(2,1)S(1)}, u32[]{:S(2)}, u32[]{:S(2)}) collective-permute-start(bf16[1,144,512]{2,1,0:T(8,128)(2,1)S(1)} %get-tuple-element.51.refs_0_.refs_10_.refs_16_), channel_id=1, source_target_pairs={{0,128},{128,0},{1,129},{129,1},{2,130},{130,2},{3,131},{131,3},{4... | collective-permute-start | bytes 442376 | tf_op jit(solution)/shard_map/ppermute | solution.py:345
  19.2 8.9 %copy-start.1 = (bf16[128,2048]{1,0:T(8,128)(2,1)}, bf16[128,2048]{1,0:T(8,128)(2,1)S(1)}, u32[]{:S(2)}) copy-start(bf16[128,2048]{1,0:T(8,128)(2,1)S(1)} %select_select_fusion.refs_3_.refs_0_) | copy-start | bytes 1572868
  20.8 6.7 %collective-permute-start.3 = (bf16[2,144,512]{2,1,0:T(8,128)(2,1)S(1)}, bf16[2,144,512]{2,1,0:T(8,128)(2,1)S(1)}, u32[]{:S(2)}, u32[]{:S(2)}) collective-permute-start(bf16[2,144,512]{2,1,0:T(8,128)(2,1)S(1)} %shard_map.100.refs_2_.refs_13_.refs_19_), channel_id=1, source_target_pairs={{0,128},{128,0},{1,129},{129,1},{2,130},{130,2},{3,131},{131,3},{4... | collective-permute-start | bytes 884744 | tf_op jit(solution)/shard_map/ppermute | solution.py:345
  22.1 5.2 %collective-permute-start.5 = (bf16[144,512]{1,0:T(8,128)(2,1)S(1)}, bf16[144,512]{1,0:T(8,128)(2,1)S(1)}, u32[]{:S(2)}, u32[]{:S(2)}) collective-permute-start(bf16[144,512]{1,0:T(8,128)(2,1)S(1)} %collective-permute-done.1.refs_0_), channel_id=1, source_target_pairs={{0,16},{16,32},{32,48},{48,64},{64,80},{80,96},{96,112},{112,0},{1... | collective-permute-start | bytes 442376 | tf_op jit(solution)/shard_map/ppermute | solution.py:345
  22.1 5.2 %collective-permute-start.6 = (bf16[144,512]{1,0:T(8,128)(2,1)S(1)}, bf16[144,512]{1,0:T(8,128)(2,1)S(1)}, u32[]{:S(2)}, u32[]{:S(2)}) collective-permute-start(bf16[144,512]{1,0:T(8,128)(2,1)S(1)} %collective-permute-done.2.refs_1_), channel_id=1, source_target_pairs={{0,112},{16,0},{32,16},{48,32},{64,48},{80,64},{96,80},{112,96},{1... | collective-permute-start | bytes 442376 | tf_op jit(solution)/shard_map/ppermute | solution.py:345
  28.1 0.7 copy-start.2
  28.8 8.9 %copy-start.3 = (bf16[2,144,512]{2,1,0:T(8,128)(2,1)S(1)}, bf16[2,144,512]{2,1,0:T(8,128)(2,1)}, u32[]{:S(2)}) copy-start(bf16[2,144,512]{2,1,0:T(8,128)(2,1)} %copy-done.2) | copy-start | bytes 884740
  28.9 8.3 %collective-permute-start.7 = (bf16[2,144,512]{2,1,0:T(8,128)(2,1)}, bf16[2,144,512]{2,1,0:T(8,128)(2,1)S(1)}, u32[]{:S(2)}, u32[]{:S(2)}) collective-permute-start(bf16[2,144,512]{2,1,0:T(8,128)(2,1)} %copy-done.2), channel_id=1, source_target_pairs={{0,128},{128,0},{1,129},{129,1},{2,130},{130,2},{3,131},{131,3},{4... | collective-permute-start | bytes 884744 | tf_op jit(solution)/shard_map/ppermute | solution.py:345
  30.2 7.0 %collective-permute-start.8 = (bf16[144,512]{1,0:T(8,128)(2,1)S(1)}, bf16[144,512]{1,0:T(8,128)(2,1)S(1)}, u32[]{:S(2)}, u32[]{:S(2)}) collective-permute-start(bf16[144,512]{1,0:T(8,128)(2,1)S(1)} %collective-permute-done.5.refs_0_), channel_id=1, source_target_pairs={{0,16},{16,32},{32,48},{48,64},{64,80},{80,96},{96,112},{112,0},{1... | collective-permute-start | bytes 442376 | tf_op jit(solution)/shard_map/ppermute | solution.py:345
  30.2 7.0 %collective-permute-start.9 = (bf16[144,512]{1,0:T(8,128)(2,1)S(1)}, bf16[144,512]{1,0:T(8,128)(2,1)S(1)}, u32[]{:S(2)}, u32[]{:S(2)}) collective-permute-start(bf16[144,512]{1,0:T(8,128)(2,1)S(1)} %collective-permute-done.6.refs_1_), channel_id=1, source_target_pairs={{0,112},{16,0},{32,16},{48,32},{64,48},{80,64},{96,80},{112,96},{1... | collective-permute-start | bytes 442376 | tf_op jit(solution)/shard_map/ppermute | solution.py:345
  33.5 16.3 %collective-permute-start.4 = (bf16[6,144,512]{2,1,0:T(8,128)(2,1)S(1)}, bf16[6,144,512]{2,1,0:T(8,128)(2,1)S(1)}, u32[]{:S(2)}, u32[]{:S(2)}) collective-permute-start(bf16[6,144,512]{2,1,0:T(8,128)(2,1)S(1)} %shard_map.101.refs_3_), channel_id=1, source_target_pairs={{0,8},{8,0},{1,9},{9,1},{2,10},{10,2},{3,11},{11,3},{4,12},{12,4},... | collective-permute-start | bytes 2654216 | tf_op jit(solution)/shard_map/ppermute | solution.py:345
  38.4 12.6 %collective-permute-start.10 = (bf16[6,144,512]{2,1,0:T(8,128)(2,1)S(1)}, bf16[6,144,512]{2,1,0:T(8,128)(2,1)S(1)}, u32[]{:S(2)}, u32[]{:S(2)}) collective-permute-start(bf16[6,144,512]{2,1,0:T(8,128)(2,1)S(1)} %shard_map.104.refs_3_), channel_id=1, source_target_pairs={{0,8},{8,0},{1,9},{9,1},{2,10},{10,2},{3,11},{11,3},{4,12},{12,4},... | collective-permute-start | bytes 2654216 | tf_op jit(solution)/shard_map/ppermute | solution.py:345
  40.9 8.9 %collective-permute-start.11 = (bf16[2,144,512]{2,1,0:T(8,128)(2,1)S(1)}, bf16[2,144,512]{2,1,0:T(8,128)(2,1)S(1)}, u32[]{:S(2)}, u32[]{:S(2)}) collective-permute-start(bf16[2,144,512]{2,1,0:T(8,128)(2,1)S(1)} %shard_map.103.refs_2_.refs_6_.refs_24_), channel_id=1, source_target_pairs={{0,128},{128,0},{1,129},{129,1},{2,130},{130,2},{3,131},{131,3},{4... | collective-permute-start | bytes 884744 | tf_op jit(solution)/shard_map/ppermute | solution.py:345
  41.4 5.5 %collective-permute-start.12 = (bf16[144,256]{1,0:T(8,128)(2,1)S(1)}, bf16[144,256]{1,0:T(8,128)(2,1)S(1)}, u32[]{:S(2)}, u32[]{:S(2)}) collective-permute-start(bf16[144,256]{1,0:T(8,128)(2,1)S(1)} %slice.136), channel_id=1, source_target_pairs={{0,16},{16,32},{32,48},{48,64},{64,80},{80,96},{96,112},{112,0},{1... | collective-permute-start | bytes 221192 | tf_op jit(solution)/shard_map/ppermute | solution.py:345
  43.9 5.8 %collective-permute-start.13 = (bf16[144,256]{1,0:T(8,128)(2,1)S(1)}, bf16[144,256]{1,0:T(8,128)(2,1)S(1)}, u32[]{:S(2)}, u32[]{:S(2)}) collective-permute-start(bf16[144,256]{1,0:T(8,128)(2,1)S(1)} %slice.137), channel_id=1, source_target_pairs={{0,112},{16,0},{32,16},{48,32},{64,48},{80,64},{96,80},{112,96},{1... | collective-permute-start | bytes 221192 | tf_op jit(solution)/shard_map/ppermute | solution.py:345
  50.3 5.1 %collective-permute-start.14 = (bf16[1,144,512]{2,1,0:T(8,128)(2,1)S(1)}, bf16[1,144,512]{2,1,0:T(8,128)(2,1)S(1)}, u32[]{:S(2)}, u32[]{:S(2)}) collective-permute-start(bf16[1,144,512]{2,1,0:T(8,128)(2,1)S(1)} %shard_map.105.refs_1_.refs_10_.refs_27_), channel_id=1, source_target_pairs={{0,128},{128,0},{1,129},{129,1},{2,130},{130,2},{3,131},{131,3},{4... | collective-permute-start | bytes 442376 | tf_op jit(solution)/shard_map/ppermute | solution.py:345
  56.0 3.2 %collective-permute-start.15 = (bf16[4,144,512]{2,1,0:T(8,128)(2,1)S(1)}, bf16[4,144,512]{2,1,0:T(8,128)(2,1)S(1)}, u32[]{:S(2)}, u32[]{:S(2)}) collective-permute-start(bf16[4,144,512]{2,1,0:T(8,128)(2,1)S(1)} %shard_map.107), channel_id=1, source_target_pairs={{0,8},{8,0},{1,9},{9,1},{2,10},{10,2},{3,11},{11,3},{4,12},{12,4},... | collective-permute-start | bytes 1769480 | tf_op jit(solution)/shard_map/ppermute | solution.py:345
  62.5 1.7 %collective-permute-start.16 = (bf16[8,32,640]{2,1,0:T(8,128)(2,1)S(1)}, bf16[8,32,640]{2,1,0:T(8,128)(2,1)S(1)}, u32[]{:S(2)}, u32[]{:S(2)}) collective-permute-start(bf16[8,32,640]{2,1,0:T(8,128)(2,1)S(1)} %get-tuple-element.23), channel_id=1, source_target_pairs={{0,8},{8,0},{1,9},{9,1},{2,10},{10,2},{3,11},{11,3},{4,12},{12,4},... | collective-permute-start | bytes 983048 | tf_op jit(solution)/shard_map/ppermute | solution.py:345
  65.4 9.8 %collective-permute-start.17 = (bf16[272,512]{1,0:T(8,128)(2,1)S(1)}, bf16[272,512]{1,0:T(8,128)(2,1)S(1)}, u32[]{:S(2)}, u32[]{:S(2)}) collective-permute-start(bf16[272,512]{1,0:T(8,128)(2,1)S(1)} %shard_map.109.refs_29_), channel_id=1, source_target_pairs={{0,128},{128,0},{1,129},{129,1},{2,130},{130,2},{3,131},{131,3},{4... | collective-permute-start | bytes 835592 | tf_op jit(solution)/shard_map/ppermute | solution.py:345
  73.0 45.7 %copy-start.4 = (f32[4096]{0:T(1024)S(1)}, f32[4096]{0:T(1024)}, u32[]{:S(2)}) copy-start(f32[4096]{0:T(1024)} %param.16) | copy-start | bytes 49156
  73.0 1.7 %collective-permute-start.18 = (bf16[4,32,640]{2,1,0:T(8,128)(2,1)S(1)}, bf16[4,32,640]{2,1,0:T(8,128)(2,1)S(1)}, u32[]{:S(2)}, u32[]{:S(2)}) collective-permute-start(bf16[4,32,640]{2,1,0:T(8,128)(2,1)S(1)} %get-tuple-element.40), channel_id=1, source_target_pairs={{0,8},{8,0},{1,9},{9,1},{2,10},{10,2},{3,11},{11,3},{4,12},{12,4},... | collective-permute-start | bytes 491528 | tf_op jit(solution)/shard_map/ppermute | solution.py:345
  73.7 1.4 collective-permute-start.19
  94.9 2.0 %collective-permute-start.20 = (bf16[32,512]{1,0:T(8,128)(2,1)S(1)}, bf16[32,512]{1,0:T(8,128)(2,1)S(1)}, u32[]{:S(2)}, u32[]{:S(2)}) collective-permute-start(bf16[32,512]{1,0:T(8,128)(2,1)S(1)} %shard_map.112), channel_id=1, source_target_pairs={{0,8},{8,0},{1,9},{9,1},{2,10},{10,2},{3,11},{11,3},{4,12},{12,4},... | collective-permute-start | bytes 98312 | tf_op jit(solution)/shard_map/ppermute | solution.py:345
  96.9 3.2 %collective-permute-start.21 = (bf16[2,32,512]{2,1,0:T(8,128)(2,1)S(1)}, bf16[2,32,512]{2,1,0:T(8,128)(2,1)S(1)}, u32[]{:S(2)}, u32[]{:S(2)}) collective-permute-start(bf16[2,32,512]{2,1,0:T(8,128)(2,1)S(1)} %pad_maximum_fusion.1.own_ref), channel_id=1, source_target_pairs={{0,128},{128,0},{1,129},{129,1},{2,130},{130,2},{3,131},{131,3},{4... | collective-permute-start | bytes 196616 | tf_op jit(solution)/shard_map/ppermute | solution.py:345
  100.9 4.0 %collective-permute-start.22 = (bf16[32,1024]{1,0:T(8,128)(2,1)S(1)}, bf16[32,1024]{1,0:T(8,128)(2,1)S(1)}, u32[]{:S(2)}, u32[]{:S(2)}) collective-permute-start(bf16[32,1024]{1,0:T(8,128)(2,1)S(1)} %get-tuple-element.28), channel_id=1, source_target_pairs={{0,2},{2,0},{4,6},{6,4},{1,3},{3,1},{5,7},{7,5},{8,10},{10,8},{12,... | collective-permute-start | bytes 196616 | tf_op jit(solution)/shard_map/ppermute | solution.py:349
  102.3 4.9 %collective-permute-start.23 = (bf16[32,1024]{1,0:T(8,128)(2,1)S(1)}, bf16[32,1024]{1,0:T(8,128)(2,1)S(1)}, u32[]{:S(2)}, u32[]{:S(2)}) collective-permute-start(bf16[32,1024]{1,0:T(8,128)(2,1)S(1)} %get-tuple-element.29), channel_id=1, source_target_pairs={{0,4},{2,6},{4,0},{6,2},{1,5},{3,7},{5,1},{7,3},{8,12},{10,14},{12... | collective-permute-start | bytes 196616 | tf_op jit(solution)/shard_map/ppermute | solution.py:349
  104.9 5.0 %collective-permute-start.24 = (bf16[32,1024]{1,0:T(8,128)(2,1)S(1)}, bf16[32,1024]{1,0:T(8,128)(2,1)S(1)}, u32[]{:S(2)}, u32[]{:S(2)}) collective-permute-start(bf16[32,1024]{1,0:T(8,128)(2,1)S(1)} %get-tuple-element.30), channel_id=1, source_target_pairs={{0,6},{2,4},{4,2},{6,0},{1,7},{3,5},{5,3},{7,1},{8,14},{10,12},{12... | collective-permute-start | bytes 196616 | tf_op jit(solution)/shard_map/ppermute | solution.py:349
  110.0 4.7 %collective-permute-start.25 = (bf16[32,1024]{1,0:T(8,128)(2,1)S(1)}, bf16[32,1024]{1,0:T(8,128)(2,1)S(1)}, u32[]{:S(2)}, u32[]{:S(2)}) collective-permute-start(bf16[32,1024]{1,0:T(8,128)(2,1)S(1)} %fusion.11), channel_id=1, source_target_pairs={{0,1},{1,0},{2,3},{3,2},{4,5},{5,4},{6,7},{7,6},{8,9},{9,8},{10,11... | collective-permute-start | bytes 196616 | tf_op jit(solution)/shard_map/ppermute | solution.py:345
  114.7 6.1 %collective-permute-start.26 = (bf16[32,1024]{1,0:T(8,128)(2,1)S(1)}, bf16[32,1024]{1,0:T(8,128)(2,1)S(1)}, u32[]{:S(2)}, u32[]{:S(2)}) collective-permute-start(bf16[32,1024]{1,0:T(8,128)(2,1)S(1)} %add_convert_fusion.own_ref), channel_id=1, source_target_pairs={{0,2},{2,0},{4,6},{6,4},{1,3},{3,1},{5,7},{7,5},{8,10},{10,8},{12,... | collective-permute-start | bytes 196616 | tf_op jit(solution)/shard_map/ppermute | solution.py:349
  114.8 6.0 %collective-permute-start.27 = (bf16[32,1024]{1,0:T(8,128)(2,1)S(1)}, bf16[32,1024]{1,0:T(8,128)(2,1)S(1)}, u32[]{:S(2)}, u32[]{:S(2)}) collective-permute-start(bf16[32,1024]{1,0:T(8,128)(2,1)S(1)} %add_convert_fusion.own_ref), channel_id=1, source_target_pairs={{0,4},{2,6},{4,0},{6,2},{1,5},{3,7},{5,1},{7,3},{8,12},{10,14},{12... | collective-permute-start | bytes 196616 | tf_op jit(solution)/shard_map/ppermute | solution.py:349
  115.8 5.0 %collective-permute-start.28 = (bf16[32,1024]{1,0:T(8,128)(2,1)S(1)}, bf16[32,1024]{1,0:T(8,128)(2,1)S(1)}, u32[]{:S(2)}, u32[]{:S(2)}) collective-permute-start(bf16[32,1024]{1,0:T(8,128)(2,1)S(1)} %add_convert_fusion.own_ref), channel_id=1, source_target_pairs={{0,6},{2,4},{4,2},{6,0},{1,7},{3,5},{5,3},{7,1},{8,14},{10,12},{12... | collective-permute-start | bytes 196616 | tf_op jit(solution)/shard_map/ppermute | solution.py:349
  122.2 6.2 %collective-permute-start.29 = (f32[2,296,128]{2,1,0:T(8,128)S(1)}, f32[2,296,128]{2,1,0:T(8,128)S(1)}, u32[]{:S(2)}, u32[]{:S(2)}) collective-permute-start(f32[2,296,128]{2,1,0:T(8,128)S(1)} %get-tuple-element.32), channel_id=1, source_target_pairs={{0,8},{8,0},{1,9},{9,1},{2,10},{10,2},{3,11},{11,3},{4,12},{12,4},... | collective-permute-start | bytes 909320 | tf_op jit(solution)/shard_map/ppermute | solution.py:345
  128.5 5.2 %collective-permute-start.30 = (f32[296,128]{1,0:T(8,128)S(1)}, f32[296,128]{1,0:T(8,128)S(1)}, u32[]{:S(2)}, u32[]{:S(2)}) collective-permute-start(f32[296,128]{1,0:T(8,128)S(1)} %dynamic-slice_bitcast_fusion), channel_id=1, source_target_pairs={{0,128},{128,0},{1,129},{129,1},{2,130},{130,2},{3,131},{131,3},{4... | collective-permute-start | bytes 454664 | tf_op jit(solution)/shard_map/ppermute | solution.py:345
  134.0 9.2 %collective-permute-start.32 = (bf16[128,256]{1,0:T(8,128)(2,1)S(1)}, bf16[128,256]{1,0:T(8,128)(2,1)S(1)}, u32[]{:S(2)}, u32[]{:S(2)}) collective-permute-start(bf16[128,256]{1,0:T(8,128)(2,1)S(1)} %pad_maximum_fusion.2), channel_id=1, source_target_pairs={{0,32},{16,48},{32,0},{48,16},{64,96},{80,112},{96,64},{112,80},{1... | collective-permute-start | bytes 196616 | tf_op jit(solution)/shard_map/ppermute | solution.py:349
  136.8 7.9 %collective-permute-start.33 = (bf16[128,256]{1,0:T(8,128)(2,1)S(1)}, bf16[128,256]{1,0:T(8,128)(2,1)S(1)}, u32[]{:S(2)}, u32[]{:S(2)}) collective-permute-start(bf16[128,256]{1,0:T(8,128)(2,1)S(1)} %pad_maximum_fusion.2), channel_id=1, source_target_pairs={{0,64},{16,80},{32,96},{48,112},{64,0},{80,16},{96,32},{112,48},{1... | collective-permute-start | bytes 196616 | tf_op jit(solution)/shard_map/ppermute | solution.py:349
  138.9 6.1 %collective-permute-start.34 = (bf16[128,256]{1,0:T(8,128)(2,1)S(1)}, bf16[128,256]{1,0:T(8,128)(2,1)S(1)}, u32[]{:S(2)}, u32[]{:S(2)}) collective-permute-start(bf16[128,256]{1,0:T(8,128)(2,1)S(1)} %pad_maximum_fusion.2), channel_id=1, source_target_pairs={{0,96},{16,112},{32,64},{48,80},{64,32},{80,48},{96,0},{112,16},{1... | collective-permute-start | bytes 196616 | tf_op jit(solution)/shard_map/ppermute | solution.py:349
  140.7 4.3 %collective-permute-start.31 = (bf16[32,128]{1,0:T(8,128)(2,1)S(1)}, bf16[32,128]{1,0:T(8,128)(2,1)S(1)}, u32[]{:S(2)}, u32[]{:S(2)}) collective-permute-start(bf16[32,128]{1,0:T(8,128)(2,1)S(1)} %fusion.19), channel_id=1, source_target_pairs={{0,16},{16,0},{32,48},{48,32},{64,80},{80,64},{96,112},{112,96},{1... | collective-permute-start | bytes 24584 | tf_op jit(solution)/shard_map/ppermute | solution.py:349
  146.1 3.3 %collective-permute-start.35 = (f32[2,2,8,256]{3,2,1,0:T(8,128)S(1)}, f32[2,2,8,256]{3,2,1,0:T(8,128)S(1)}, u32[]{:S(2)}, u32[]{:S(2)}) collective-permute-start(f32[2,2,8,256]{3,2,1,0:T(8,128)S(1)} %get-tuple-element.59), channel_id=1, source_target_pairs={{0,8},{8,0},{1,9},{9,1},{2,10},{10,2},{3,11},{11,3},{4,12},{12,4},... | collective-permute-start | bytes 98312 | tf_op jit(solution)/shard_map/ppermute | solution.py:345
  149.4 3.0 %collective-permute-start.36 = (f32[2,8,256]{2,1,0:T(8,128)S(1)}, f32[2,8,256]{2,1,0:T(8,128)S(1)}, u32[]{:S(2)}, u32[]{:S(2)}) collective-permute-start(f32[2,8,256]{2,1,0:T(8,128)S(1)} %get-tuple-element.62), channel_id=1, source_target_pairs={{0,128},{128,0},{1,129},{129,1},{2,130},{130,2},{3,131},{131,3},{4... | collective-permute-start | bytes 49160 | tf_op jit(solution)/shard_map/ppermute | solution.py:345
  150.5 3.0 %collective-permute-start.37 = (f32[2,8,256]{2,1,0:T(8,128)S(1)}, f32[2,8,256]{2,1,0:T(8,128)S(1)}, u32[]{:S(2)}, u32[]{:S(2)}) collective-permute-start(f32[2,8,256]{2,1,0:T(8,128)S(1)} %get-tuple-element.61), channel_id=1, source_target_pairs={{0,16},{16,0},{32,48},{48,32},{64,80},{80,64},{96,112},{112,96},{1... | collective-permute-start | bytes 49160 | tf_op jit(solution)/shard_map/ppermute | solution.py:349
  152.4 3.5 %collective-permute-start.38 = (f32[2,8,256]{2,1,0:T(8,128)S(1)}, f32[2,8,256]{2,1,0:T(8,128)S(1)}, u32[]{:S(2)}, u32[]{:S(2)}) collective-permute-start(f32[2,8,256]{2,1,0:T(8,128)S(1)} %get-tuple-element.63), channel_id=1, source_target_pairs={{0,144},{16,128},{32,176},{48,160},{64,208},{80,192},{96,240},{112... | collective-permute-start | bytes 49160 | tf_op jit(solution)/shard_map/ppermute | solution.py:528
Sparse Core Ops, SparseCore 0:
  29.0 59.8 all-gather.1
